TPU v7x, 32 devices: a whole 2x2x4 slice. The times are simulated.
32 devices in a mesh: dp: 8 (over y, x, core), rep: 4 (over z).
Axes of the slice: x: 2, y: 2, z: 4, core: 2. Of those that a mesh axis runs over, the one named last changes fastest.
Arguments:
- tokens: bfloat16 [2, 6144, 768], P(None, ('dp', 'rep')), may hold values from -6 to 6
- positions: int32 [64, 96], P(('dp', 'rep')), may hold values from 0 to 95, each once within a row
- missing: int32 [64], replicated, may hold values 0 or 1
- qkv_weight: bfloat16 [2, 768, 2304], replicated, may hold values from -0.21875 to 0.21875
- out_weight: bfloat16 [2, 768, 768], replicated, may hold values from -0.625 to 0.625
- up_weight: bfloat16 [2, 768, 3072], replicated, may hold values from -0.21875 to 0.21875
- down_weight: bfloat16 [2, 3072, 768], replicated, may hold values from -0.109375 to 0.109375
- norm_gains: float32 [2, 2, 768], replicated, may hold values from 0.5 to 1.5
Outputs:
- loss_value: float32 [], replicated
- token_grads: float32 [2, 6144, 768], P(None, ('dp', 'rep'))
- qkv_grads: float32 [2, 768, 2304], P(None, 'dp')
- out_grads: float32 [2, 768, 768], P(None, 'dp')
- up_grads: float32 [2, 768, 3072], P(None, 'dp')
- down_grads: float32 [2, 3072, 768], P(None, 'dp')
- gain_grads: float32 [2, 2, 768], P(None, None, 'dp')
Inputs may be any that keep to these rules, and one draw needn't show every extreme that they name: Each image's 96 positions name every cell of a 8 by 12 grid once.
All inputs are finite; a program needn't handle non-finite values.
Results may differ from a plain program's by a relative error of at most 0.018.
Values may be sent and summed in bfloat16 or wider, within the bound.
A program may use at most 256 MiB of HBM per device.

v0:
```python
import jax
import jax.numpy as jnp
from jax import lax
from jax.sharding import PartitionSpec as P

HEADS = 12
GRID_W = 12


eps_norm = 1e-06
inv_temp = 32.0


def lead_dot(left, right):
    return lax.dot_general(
        left, right, (((0,), (0,)), ((), ())), preferred_element_type=jnp.float32
    )


def tail_dot(left, right):
    return lax.dot_general(
        left, right, (((1,), (1,)), ((), ())), preferred_element_type=jnp.float32
    )


def norm_gain(values, gain):
    centre = values - jnp.mean(values, axis=-1, keepdims=True)
    spread = jnp.mean(centre * centre, axis=-1, keepdims=True)
    return centre * lax.rsqrt(spread + eps_norm) * gain


def unit_rows(pooled):
    return pooled * lax.rsqrt(jnp.sum(pooled * pooled, axis=1, keepdims=True) + eps_norm)


def gelu_exact(values):
    return jax.nn.gelu(values, approximate=False)


def alibi_bias(positions):
    grid_rows = (positions // GRID_W).astype(jnp.float32)
    grid_cols = (positions % GRID_W).astype(jnp.float32)
    row_gap = grid_rows[:, :, None] - grid_rows[:, None, :]
    col_gap = grid_cols[:, :, None] - grid_cols[:, None, :]
    distance = jnp.sqrt(row_gap * row_gap + col_gap * col_gap)
    slopes = jnp.exp2(-8.0 * (jnp.arange(HEADS) + 1).astype(jnp.float32) / HEADS)
    return -slopes[None, :, None, None] * distance[:, None, :, :]


def log_total(logits, valid_cols, valid_rows):
    row_max = jnp.max(logits, axis=1, keepdims=True)
    summed = jnp.sum(valid_cols[None, :] * jnp.exp(logits - row_max), axis=1) + (1.0 - valid_rows)
    return row_max[:, 0] + jnp.log(summed)


def row_grads(logits, log_sums, valid_rows, valid_cols, match, total_items):
    soft = valid_cols[None, :] * jnp.exp(logits - log_sums[:, None])
    return (valid_rows[:, None] / (2.0 * total_items) * (soft - match)).astype(jnp.bfloat16)


def block_forward(token_rows, alibi_terms, qkv_weight, out_weight, up_weight, down_weight, gains):
    row_count, model_width = token_rows.shape
    images, patches = (alibi_terms.shape[0], alibi_terms.shape[2])
    head_dim = model_width // HEADS
    score_scale = head_dim ** (-0.5)
    start_rows = token_rows.astype(jnp.float32)
    normed_one = norm_gain(start_rows, gains[0]).astype(jnp.bfloat16)
    projected = jnp.dot(normed_one, qkv_weight, preferred_element_type=jnp.float32).astype(
        jnp.bfloat16
    )
    queries = projected[:, :model_width].reshape(images, patches, HEADS, head_dim)
    key_rows = projected[:, model_width : 2 * model_width].reshape(images, patches, HEADS, head_dim)
    value_rows = projected[:, 2 * model_width :].reshape(images, patches, HEADS, head_dim)
    scores = jnp.einsum("iqhd,ikhd->ihqk", queries, key_rows, preferred_element_type=jnp.float32)
    attn_probs = jax.nn.softmax(scores * score_scale + alibi_terms, axis=-1)
    probs_low = attn_probs.astype(jnp.bfloat16)
    attended = jnp.einsum(
        "ihqk,ikhd->iqhd", probs_low, value_rows, preferred_element_type=jnp.float32
    )
    attended = attended.reshape(row_count, model_width).astype(jnp.bfloat16)
    residual = start_rows + jnp.dot(attended, out_weight, preferred_element_type=jnp.float32)
    normed_two = norm_gain(residual, gains[1]).astype(jnp.bfloat16)
    hidden_pre = jnp.dot(normed_two, up_weight, preferred_element_type=jnp.float32)
    active = gelu_exact(hidden_pre).astype(jnp.bfloat16)
    out_rows = residual + jnp.dot(active, down_weight, preferred_element_type=jnp.float32)
    saved = (
        start_rows,
        normed_one,
        projected,
        attn_probs,
        probs_low,
        attended,
        residual,
        normed_two,
        hidden_pre,
        active,
    )
    return (out_rows, saved)


def block_backward(grad_rows, saved, qkv_weight, out_weight, up_weight, down_weight, gains):
    (
        start_rows,
        normed_one,
        projected,
        attn_probs,
        probs_low,
        attended,
        residual,
        normed_two,
        hidden_pre,
        active,
    ) = saved
    images, head_count, patches = (attn_probs.shape[0], attn_probs.shape[1], attn_probs.shape[2])
    row_count, model_width = grad_rows.shape
    head_dim = model_width // head_count
    score_scale = head_dim ** (-0.5)
    down_in = grad_rows.astype(jnp.bfloat16)
    grad_down = lead_dot(active, down_in)
    grad_active = tail_dot(down_in, down_weight)
    _, gelu_back = jax.vjp(gelu_exact, hidden_pre)
    grad_hidden = gelu_back(grad_active)[0].astype(jnp.bfloat16)
    grad_up = lead_dot(normed_two, grad_hidden)
    grad_h_two = tail_dot(grad_hidden, up_weight)
    _, norm_two_back = jax.vjp(norm_gain, residual, gains[1])
    grad_mid, gain_two = norm_two_back(grad_h_two)
    grad_residual = grad_rows + grad_mid
    attn_in = grad_residual.astype(jnp.bfloat16)
    grad_out = lead_dot(attended, attn_in)
    grad_att = (
        tail_dot(attn_in, out_weight)
        .astype(jnp.bfloat16)
        .reshape(images, patches, head_count, head_dim)
    )
    queries = projected[:, :model_width].reshape(images, patches, head_count, head_dim)
    key_rows = projected[:, model_width : 2 * model_width].reshape(
        images, patches, head_count, head_dim
    )
    value_rows = projected[:, 2 * model_width :].reshape(images, patches, head_count, head_dim)
    grad_values = jnp.einsum(
        "ihqk,iqhd->ikhd", probs_low, grad_att, preferred_element_type=jnp.float32
    )
    grad_probs = jnp.einsum(
        "iqhd,ikhd->ihqk", grad_att, value_rows, preferred_element_type=jnp.float32
    )
    grad_scores = attn_probs * (
        grad_probs - jnp.sum(grad_probs * attn_probs, axis=-1, keepdims=True)
    )
    grad_scores = grad_scores.astype(jnp.bfloat16)
    grad_queries = (
        jnp.einsum("ihqk,ikhd->iqhd", grad_scores, key_rows, preferred_element_type=jnp.float32)
        * score_scale
    )
    grad_keys = (
        jnp.einsum("ihqk,iqhd->ikhd", grad_scores, queries, preferred_element_type=jnp.float32)
        * score_scale
    )
    grad_proj = jnp.concatenate(
        [
            grad_queries.reshape(row_count, model_width),
            grad_keys.reshape(row_count, model_width),
            grad_values.reshape(row_count, model_width),
        ],
        axis=1,
    ).astype(jnp.bfloat16)
    grad_qkv = lead_dot(normed_one, grad_proj)
    grad_h_one = tail_dot(grad_proj, qkv_weight)
    _, norm_one_back = jax.vjp(norm_gain, start_rows, gains[0])
    grad_first, gain_one = norm_one_back(grad_h_one)
    weight_grads = (grad_qkv, grad_out, grad_up, grad_down, jnp.stack([gain_one, gain_two]))
    return (grad_residual + grad_first, weight_grads)


def local(tokens, positions, missing, qkv_weight, out_weight, up_weight, down_weight, norm_gains):
    own_images = positions.shape[0]
    model_width = tokens.shape[2]
    patches = tokens.shape[1] // own_images
    first_row = lax.axis_index(("dp", "rep")) * own_images
    alibi_terms = alibi_bias(positions)
    saved_list = []
    pooled_list = []
    normed = []
    for modality in range(2):
        out_rows, saved = block_forward(
            tokens[modality],
            alibi_terms,
            qkv_weight[modality],
            out_weight[modality],
            up_weight[modality],
            down_weight[modality],
            norm_gains[modality],
        )
        pooled = jnp.sum(out_rows.reshape(own_images, patches, model_width), axis=1)
        saved_list.append(saved)
        pooled_list.append(pooled)
        normed.append(unit_rows(pooled).astype(jnp.bfloat16))
    valid_all = 1.0 - missing.astype(jnp.float32)
    total_items = float(missing.shape[0])
    valid_own = lax.dynamic_slice_in_dim(valid_all, first_row, own_images)
    radar_all, optic_all = (
        lax.all_gather(normed[0], ("dp", "rep"), axis=0, tiled=True),
        lax.all_gather(normed[1], ("dp", "rep"), axis=0, tiled=True),
    )
    images_all = radar_all.shape[0]
    match_own = (
        lax.broadcasted_iota(jnp.int32, (own_images, images_all), 0) + first_row
        == lax.broadcasted_iota(jnp.int32, (own_images, images_all), 1)
    ).astype(jnp.float32)
    logits_r = tail_dot(normed[0], optic_all) * inv_temp
    logits_o = tail_dot(normed[1], radar_all) * inv_temp
    lse_r = log_total(logits_r, valid_all, valid_own)
    lse_o = log_total(logits_o, valid_all, valid_own)
    item_terms = valid_own * (
        lse_r
        - jnp.sum(logits_r * match_own, axis=1)
        + lse_o
        - jnp.sum(logits_o * match_own, axis=1)
    )
    grad_lr = row_grads(logits_r, lse_r, valid_own, valid_all, match_own, total_items)
    grad_lo = row_grads(logits_o, lse_o, valid_own, valid_all, match_own, total_items)
    grad_ur = jnp.dot(grad_lr, optic_all, preferred_element_type=jnp.float32) * inv_temp
    grad_uo = jnp.dot(grad_lo, radar_all, preferred_element_type=jnp.float32) * inv_temp
    summed_terms = lax.psum(jnp.sum(item_terms), ("dp", "rep"))
    loss_value = summed_terms / (2.0 * total_items)
    share_o = lead_dot(grad_lr, normed[0]) * inv_temp
    share_r = lead_dot(grad_lo, normed[1]) * inv_temp
    back_r, back_o = (
        lax.psum_scatter(share_r, ("dp", "rep"), scatter_dimension=0, tiled=True),
        lax.psum_scatter(share_o, ("dp", "rep"), scatter_dimension=0, tiled=True),
    )
    grad_ur = grad_ur + back_r
    grad_uo = grad_uo + back_o
    grad_units = (grad_ur, grad_uo)
    token_list = []
    block_grads = []
    for modality in range(2):
        _, unit_back = jax.vjp(unit_rows, pooled_list[modality])
        grad_pooled = unit_back(grad_units[modality])[0]
        grad_rows = jnp.broadcast_to(grad_pooled[:, None, :], (own_images, patches, model_width))
        grad_rows = grad_rows.reshape(own_images * patches, model_width)
        grad_tokens, weight_grads = block_backward(
            grad_rows,
            saved_list[modality],
            qkv_weight[modality],
            out_weight[modality],
            up_weight[modality],
            down_weight[modality],
            norm_gains[modality],
        )
        token_list.append(grad_tokens)
        block_grads.append(list(weight_grads))
    stacked = [jnp.stack([block_grads[0][slot], block_grads[1][slot]]) for slot in range(5)]
    shares = (
        lax.psum_scatter(stacked[0], "dp", scatter_dimension=1, tiled=True),
        lax.psum_scatter(stacked[1], "dp", scatter_dimension=1, tiled=True),
        lax.psum_scatter(stacked[2], "dp", scatter_dimension=1, tiled=True),
        lax.psum_scatter(stacked[3], "dp", scatter_dimension=1, tiled=True),
        lax.psum_scatter(stacked[4], "dp", scatter_dimension=2, tiled=True),
    )
    summed = (
        lax.psum(shares[0].astype(jnp.bfloat16), "rep").astype(jnp.float32),
        lax.psum(shares[1].astype(jnp.bfloat16), "rep").astype(jnp.float32),
        lax.psum(shares[2].astype(jnp.bfloat16), "rep").astype(jnp.float32),
        lax.psum(shares[3].astype(jnp.bfloat16), "rep").astype(jnp.float32),
        lax.psum(shares[4].astype(jnp.bfloat16), "rep").astype(jnp.float32),
    )
    stacked = list(summed)
    token_grads = jnp.stack(token_list)
    return (loss_value, token_grads, stacked[0], stacked[1], stacked[2], stacked[3], stacked[4])


def solution(mesh):
    in_specs = (P(None, ("dp", "rep"), None), P(("dp", "rep"), None), P(), P(), P(), P(), P(), P())
    out_specs = (
        P(),
        P(None, ("dp", "rep"), None),
        P(None, "dp", None),
        P(None, "dp", None),
        P(None, "dp", None),
        P(None, "dp", None),
        P(None, None, "dp"),
    )
    return jax.shard_map(local, mesh=mesh, in_specs=in_specs, out_specs=out_specs, check_vma=False)
```

profile of v0, /device:TPU:0, one launch (start us, length us, event | category | flops | bytes accessed | tf_op | source)
XLA Modules:
  0.0 959.6 jit_solution(5256350842321347427)
XLA Ops:
  8.7 1.2 convert_reduce_fusion.1
  10.0 1.4 fusion.104
  11.4 3.0 convolution_convert_fusion.1
  20.0 1.9 fusion.171
  22.2 9.0 multiply_convert_fusion.1
  33.2 70.6 %all-gather.1 = bf16[32,2,768]{2,1,0:T(2,128)(2,1)S(1)} all-gather(bf16[1,2,768]{2,1,0:T(2,128)(2,1)S(1)} %fusion.227), channel_id=1, replica_groups=mesh['dp'=8,'rep'=4] {'dp','rep'}, dimensions={0}, use_global_device_ids=true | all-gather | bytes 101376 | tf_op jit(solution)/shard_map/all_gather | solution.py:201
  103.9 2.9 convolution_convert_fusion
  107.4 1.3 copy.92
  110.8 2.6 fusion.168
  113.4 1.7 fusion.71
  115.8 2.0 fusion.169
  118.1 9.1 multiply_convert_fusion
  128.9 64.1 %all-gather = bf16[32,2,768]{2,1,0:T(2,128)(2,1)S(1)} all-gather(bf16[1,2,768]{2,1,0:T(2,128)(2,1)S(1)} %fusion.226), channel_id=1, replica_groups=mesh['dp'=8,'rep'=4] {'dp','rep'}, dimensions={0}, use_global_device_ids=true | all-gather | bytes 101376 | tf_op jit(solution)/shard_map/all_gather | solution.py:202
  196.7 125.7 %all-reduce.7.cloned.1.call-done = (f32[64,768]{1,0:T(8,128)}, f32[64,768]{1,0:T(8,128)}) async-done(((f32[64,768]{1,0:T(8,128)}, f32[64,768]{1,0:T(8,128)}), (f32[64,768]{1,0:T(8,128)}, f32[64,768]{1,0:T(8,128)})) %all-reduce.7.cloned.1.call-update) | async-done | bytes 393232
  323.7 5.8 add_convert_fusion.1
  329.5 5.9 multiply_reduce_fusion.3
  336.7 2.2 add_convert_fusion
  339.0 2.5 multiply_reduce_fusion.2
  344.5 2.4 pad_maximum_fusion.3
  347.8 1.8 convolution_convert_fusion.7
  349.7 1.4 reshape.350
  351.1 1.7 copy.96
  352.8 2.1 multiply_reduce_fusion.1
  356.3 1.2 copy.100
  357.4 2.1 reshape.326
  359.5 1.5 fusion.68
  362.4 1.9 fusion.72
  365.7 2.7 convolution_convert_fusion.6
  368.4 2.4 reshape.351
  370.8 2.4 copy.108
  373.2 1.9 multiply_reduce_fusion
  376.4 1.2 copy.112
  377.5 2.0 reshape.331
  379.5 1.5 fusion.66
  382.4 1.9 fusion.73
  384.2 1.2 copy.118
  385.4 2.0 reshape.333
  387.4 1.1 constant_dynamic-update-slice_fusion.5
  389.8 4.2 convolution_bitcast_fusion.4
  394.0 4.2 convolution_bitcast_fusion.5
  398.2 11.2 %pad_maximum_fusion.2 = f32[2,768,2304]{2,1,0:T(8,128)} fusion(f32[1,768,2304]{2,1,0:T(8,128)} %convolution_bitcast_fusion.4, f32[1,768,2304]{2,1,0:T(8,128)} %convolution_bitcast_fusion.5), kind=kLoop, calls=%fused_computation.4 | loop fusion | flops 3538944 | bytes 28311552 | tf_op jit(solution)/shard_map/stack | solution.py:252
  410.1 2.9 convolution_bitcast_fusion.2
  413.0 1.5 convolution_bitcast_fusion.3
  414.6 10.7 %pad_maximum_fusion = f32[2,768,3072]{2,1,0:T(8,128)} fusion(f32[1,768,3072]{2,1,0:T(8,128)S(1)} %convolution_bitcast_fusion.2, f32[1,768,3072]{2,1,0:T(8,128)S(1)} %convolution_bitcast_fusion.3), kind=kLoop, calls=%fused_computation.2 | loop fusion | flops 4718592 | bytes 37748736 | tf_op jit(solution)/shard_map/stack | solution.py:252
  426.1 3.2 convolution_bitcast_fusion
  429.3 1.5 convolution_bitcast_fusion.1
  430.7 6.9 pad_maximum_fusion.1
  438.3 5.0 fusion.105
  443.4 3.5 fusion.99
  447.0 1.1 fusion.101
  448.7 1.2 reshape.342
  450.0 1.8 convert_element_type.228
  451.8 57.8 %reduce-scatter.8.cloned.1.call-done = f32[2,96,2304]{2,1,0:T(8,128)} async-done(((f32[2,768,2304]{2,1,0:T(8,128)}), f32[2,96,2304]{2,1,0:T(8,128)}) %reduce-scatter.8.cloned.1.call-update) | async-done | bytes 1769488 | tf_op jit(solution)/shard_map/reduce_scatter | solution.py:254
  509.7 2.5 convert_element_type.226
  512.1 127.1 %reduce-scatter.12.cloned.1.call-done = f32[2,96,3072]{2,1,0:T(8,128)} async-done(((f32[2,768,3072]{2,1,0:T(8,128)}), f32[2,96,3072]{2,1,0:T(8,128)}) %reduce-scatter.12.cloned.1.call-update) | async-done | bytes 2359312 | tf_op jit(solution)/shard_map/reduce_scatter | solution.py:256
  639.3 2.8 convert_element_type.230
  642.1 126.8 %reduce-scatter.14.cloned.1.call-done = f32[2,384,768]{2,1,0:T(8,128)} async-done(((f32[2,3072,768]{2,1,0:T(8,128)}), f32[2,384,768]{2,1,0:T(8,128)}) %reduce-scatter.14.cloned.1.call-update) | async-done | bytes 2359312 | tf_op jit(solution)/shard_map/reduce_scatter | solution.py:257
  768.8 2.8 convert_element_type.234
  771.7 39.6 %psum.42 = f32[]{:T(128)} all-reduce(f32[]{:T(128)} %get-tuple-element.46), channel_id=1, replica_groups=mesh['dp'=8,'rep'=4] {'dp','rep'}, use_global_device_ids=true, to_apply=%region_23.24 | all-reduce | flops 1 | bytes 8 | tf_op jit(solution)/shard_map/psum | solution.py:223
  814.4 11.6 %psum.47 = bf16[2,2,96]{2,1,0:T(2,128)(2,1)S(1)} all-reduce(bf16[2,2,96]{2,1,0:T(2,128)(2,1)S(1)} %copy.128), channel_id=1, replica_groups=mesh['dp'=8,'rep'=4] {'rep'}, use_global_device_ids=true, to_apply=%region_51.52 | all-reduce | flops 384 | bytes 1536 | tf_op jit(solution)/shard_map/psum | solution.py:265
  826.6 117.9 %all-reduce.9.cloned.1.call-done = (bf16[2,96,2304]{2,1,0:T(8,128)(2,1)}, bf16[2,96,768]{2,1,0:T(8,128)(2,1)}, bf16[2,96,3072]{2,1,0:T(8,128)(2,1)}, bf16[2,384,768]{2,1,0:T(8,128)(2,1)}) async-done(((bf16[2,96,2304]{2,1,0:T(8,128)(2,1)}, bf16[2,96,768]{2,1,0:T(8,128)(2,1)}, bf16[2,96,3072]{2,1,0:T(8,128)(2,1)}, bf16[2,384,768]{2,1,0:T(8,128)(2,1)}), (bf16[2,96,2304]{2,1,0:T(8,128)(2,1)}, ...) | async-done | bytes 3538960 | tf_op jit(solution)/shard_map/psum | solution.py:261
  944.5 2.6 convert_element_type.227
  948.0 1.7 convert_element_type.231
  949.6 1.6 convert_element_type.235
  (320 shorter events, 38.8 us)
Async XLA Ops:
  7.2 315.3 %all-reduce.7.cloned.1.call-start = ((), (), s32[]{:S(2)}) async-start(), calls=%async_computation.10 | async-start | bytes 786432
  9.9 4.5 copy-start.52
  9.9 94.0 %copy-start.40 = (f32[192]{0:T(256)}, f32[192]{0:T(256)S(1)}, u32[]{:S(2)}) copy-start(f32[192]{0:T(256)S(1)} %broadcast_multiply_fusion.1) | copy-start | bytes 2308
  11.3 3.1 copy-start.71
  11.3 92.6 %copy-start.69 = (f32[192]{0:T(256)}, f32[192]{0:T(256)S(1)}, u32[]{:S(2)}) copy-start(f32[192]{0:T(256)S(1)} %get-tuple-element.17) | copy-start | bytes 2308
  11.4 3.1 copy-start.64
  15.5 3.0 copy-start.30
  20.0 11.3 %slice-start = ((s8[9437184]{0:T(1024)(128)(4,1)}), s8[4194304]{0:T(1024)(128)(4,1)S(1)}, s32[]{:S(2)}) async-start(s8[9437184]{0:T(1024)(128)(4,1)} %bitcast.274), calls=%async_computation.12 | async-start | bytes 8388608
  22.0 319.5 %copy-start.44 = (f32[192]{0:T(256)}, f32[192]{0:T(256)S(1)}, u32[]{:S(2)}) copy-start(f32[192]{0:T(256)S(1)} %broadcast_multiply_fusion.2) | copy-start | bytes 2308
  22.2 319.3 %copy-start.60 = (f32[192]{0:T(256)}, f32[192]{0:T(256)S(1)}, u32[]{:S(2)}) copy-start(f32[192]{0:T(256)S(1)} %fusion.147) | copy-start | bytes 2308
  22.2 9.1 slice-start.1
  22.2 9.1 slice-start.2
  103.9 3.0 copy-start.48
  109.7 3.7 copy-start.16
  110.8 4.4 copy-start.17
  115.8 11.3 %copy-start.7 = (bf16[192,768]{0,1:T(8,128)(2,1)}, bf16[192,768]{0,1:T(8,128)(2,1)S(1)}, u32[]{:S(2)}) copy-start(bf16[192,768]{0,1:T(8,128)(2,1)S(1)} %convert_element_type.205) | copy-start | bytes 884740
  115.8 11.3 %slice-start.3 = ((s8[9437184]{0:T(1024)(128)(4,1)}), s8[4194304]{0:T(1024)(128)(4,1)S(1)}, s32[]{:S(2)}) async-start(s8[9437184]{0:T(1024)(128)(4,1)} %bitcast.276), calls=%async_computation.15 | async-start | bytes 8388608
  117.8 223.7 %copy-start.46 = (f32[192]{0:T(256)}, f32[192]{0:T(256)S(1)}, u32[]{:S(2)}) copy-start(f32[192]{0:T(256)S(1)} %broadcast_multiply_fusion) | copy-start | bytes 2308
  118.0 223.4 %copy-start.62 = (f32[192]{0:T(256)}, f32[192]{0:T(256)S(1)}, u32[]{:S(2)}) copy-start(f32[192]{0:T(256)S(1)} %fusion.149) | copy-start | bytes 2308
  118.0 9.1 slice-start.4
  118.1 9.1 slice-start.5
  127.2 196.3 %copy-start.82 = (f32[2]{0:T(128)S(1)}, f32[2]{0:T(128)}, u32[]{:S(2)}) copy-start(f32[2]{0:T(128)} %copy-done.81) | copy-start | bytes 28
  196.2 253.8 %reduce-scatter.10.cloned.1.call-start = ((), (), s32[]{:S(2)}) async-start(), calls=%async_computation.6 | async-start | bytes 5308416 | tf_op jit(solution)/shard_map/reduce_scatter | solution.py:255
  323.6 19.3 %copy-start.34 = (f32[2,768]{1,0:T(2,128)}, f32[2,768]{1,0:T(2,128)S(1)}, u32[]{:S(2)}) copy-start(f32[2,768]{1,0:T(2,128)S(1)} %get-tuple-element.39) | copy-start | bytes 18436
  323.6 13.0 %slice-start.6 = ((s8[9437184]{0:T(1024)(128)(4,1)}), s8[4194304]{0:T(1024)(128)(4,1)S(1)}, s32[]{:S(2)}) async-start(s8[9437184]{0:T(1024)(128)(4,1)} %bitcast.278), calls=%async_computation.18 | async-start | bytes 8388608
  323.6 13.0 %slice-start.7 = ((s8[9437184]{0:T(1024)(128)(4,1)}), s8[4194304]{0:T(1024)(128)(4,1)S(1)}, s32[]{:S(2)}) async-start(s8[9437184]{0:T(1024)(128)(4,1)} %bitcast.278), calls=%async_computation.19 | async-start | bytes 8388608
  323.6 13.0 %copy-start.83 = (f32[192,3072]{1,0:T(8,128)S(1)}, f32[192,3072]{1,0:T(8,128)}, u32[]{:S(2)}) copy-start(f32[192,3072]{1,0:T(8,128)} %get-tuple-element.52) | copy-start | bytes 7077892
  323.6 13.0 %copy-start.84 = (f32[192,3072]{1,0:T(8,128)S(1)}, f32[192,3072]{1,0:T(8,128)}, u32[]{:S(2)}) copy-start(f32[192,3072]{1,0:T(8,128)} %get-tuple-element.66) | copy-start | bytes 7077892
  329.4 6.0 copy-start.19
  329.4 7.2 slice-start.8
  329.4 9.5 slice-start.9
  329.5 9.5 slice-start.10
  336.5 5.4 copy-start.37
  346.9 162.7 %reduce-scatter.8.cloned.1.call-start = ((), (), s32[]{:S(2)}) async-start(), calls=%async_computation.5 | async-start | bytes 15925248 | tf_op jit(solution)/shard_map/reduce_scatter | solution.py:254
  365.7 7.4 copy-start.31
  365.7 7.4 copy-start.58
  382.4 5.0 copy-start.9
  389.6 4.3 copy-start.3
  389.7 4.2 copy-start.1
  389.7 4.2 copy-start.53
  389.8 4.2 copy-start.65
  409.5 3.6 copy-start.45
  409.5 3.6 copy-start.61
  409.5 229.8 %reduce-scatter.12.cloned.1.call-start = ((), (), s32[]{:S(2)}) async-start(), calls=%async_computation.7 | async-start | bytes 21233664 | tf_op jit(solution)/shard_map/reduce_scatter | solution.py:256
  410.1 2.9 copy-start.20
  425.4 343.5 %reduce-scatter.14.cloned.1.call-start = ((), (), s32[]{:S(2)}) async-start(), calls=%async_computation.8 | async-start | bytes 21233664 | tf_op jit(solution)/shard_map/reduce_scatter | solution.py:257
  426.1 3.2 copy-start.5
  437.7 375.8 %reduce-scatter.16.cloned.1.call-start = ((), (), s32[]{:S(2)}) async-start(), calls=%async_computation.9 | async-start | bytes 442368
  438.3 5.0 copy-start.72
  438.3 5.0 copy-start.2
  443.3 3.6 copy-start.70
  443.3 3.6 copy-start.42
  443.4 3.6 copy-start.50
  443.4 3.6 copy-start.54
  443.4 3.6 copy-start.66
  443.4 3.6 copy-start.76
  449.9 494.6 %all-reduce.9.cloned.1.call-start = ((), (), s32[]{:S(2)}) async-start(), calls=%async_computation.11 | async-start | bytes 7077888 | tf_op jit(solution)/shard_map/psum | solution.py:261
  771.6 40.3 %copy-start.77 = (f32[192]{0:T(256)S(1)}, f32[192]{0:T(256)}, u32[]{:S(2)}) copy-start(f32[192]{0:T(256)} %get-tuple-element.10) | copy-start | bytes 2308
  771.6 40.3 %copy-start.39 = (f32[2,768]{1,0:T(2,128)S(1)}, f32[2,768]{1,0:T(2,128)}, u32[]{:S(2)}) copy-start(f32[2,768]{1,0:T(2,128)} %copy-done.37) | copy-start | bytes 18436
  771.6 40.3 %copy-start.43 = (f32[192]{0:T(256)S(1)}, f32[192]{0:T(256)}, u32[]{:S(2)}) copy-start(f32[192]{0:T(256)} %copy-done.40) | copy-start | bytes 2308
  771.6 40.4 %copy-start.51 = (f32[192]{0:T(256)S(1)}, f32[192]{0:T(256)}, u32[]{:S(2)}) copy-start(f32[192]{0:T(256)} %copy-done.48) | copy-start | bytes 2308
  771.6 40.4 %copy-start.68 = (f32[192]{0:T(256)S(1)}, f32[192]{0:T(256)}, u32[]{:S(2)}) copy-start(f32[192]{0:T(256)} %copy-done.67) | copy-start | bytes 2308
  771.7 40.4 %copy-start.74 = (f32[192]{0:T(256)S(1)}, f32[192]{0:T(256)}, u32[]{:S(2)}) copy-start(f32[192]{0:T(256)} %copy-done.73) | copy-start | bytes 2308
  944.5 3.5 copy-start.23
  (40 other events, 60.1 us)
Sparse Core Ops, SparseCore 0:
  196.3 126.0 all-reduce.6
  347.0 52.9 reduce-scatter.9
  409.6 100.0 reduce-scatter.7
  513.1 126.0 reduce-scatter.11
  642.7 126.0 reduce-scatter.13
  772.3 33.8 reduce-scatter.15
  809.4 135.0 all-reduce.8
where the time goes:
time: 969 us; the launch traced here: 960 us
  waiting for transfers between devices  555 us (57%)
  blocking collectives  186 us (19%)
  matrix products  99.2 us (10%)
  other arithmetic  57.7 us (6%)
  local copies, waits for them, and re-layouts  42.4 us (4%)
  between operations  18 us (2%)
    reduce_scatter x1, waiting for transfers between devices, local(): lax.psum_scatter(stacked[2], 'dp', scatter_dimension=1, tiled=True)  127 us
    reduce_scatter x1, waiting for transfers between devices, local(): lax.psum_scatter(stacked[3], 'dp', scatter_dimension=1, tiled=True)  127 us
    unnamed x9, waiting for transfers between devices  126 us
    psum x1, waiting for transfers between devices, local(): lax.psum(shares[0].astype(jnp.bfloat16), 'rep').astype(jnp.float32)  118 us
    all_gather x1, blocking collectives, local(): lax.all_gather(normed[0], ('dp', 'rep'), axis=0, tiled=True)  70.6 us
    all_gather x1, blocking collectives, local(): lax.all_gather(normed[1], ('dp', 'rep'), axis=0, tiled=True)  64.1 us
    reduce_scatter x1, waiting for transfers between devices, local(): lax.psum_scatter(stacked[0], 'dp', scatter_dimension=1, tiled=True)  57.8 us
    psum x1, blocking collectives, local(): summed_terms = lax.psum(jnp.sum(item_terms), ('dp', 'rep'))  39.6 us
  transfers between devices with their start and end apart: 7, of which 5 were waited for; matrix products, arithmetic and copies ran while one was open for 12% of the time, Pallas kernels for 0%

commit v1 on v0

--- a/solution.py
+++ b/solution.py
@@ -1,14 +1,694 @@
+import functools
+
 import jax
 import jax.numpy as jnp
 from jax import lax
+from jax.experimental import pallas as pl
+from jax.experimental.pallas import tpu as pltpu
 from jax.sharding import PartitionSpec as P
 
 HEADS = 12
 GRID_W = 12
-
+MESH = pl.DeviceIdType.MESH
+F32 = jnp.float32
+BF16 = jnp.bfloat16
 
 eps_norm = 1e-06
 inv_temp = 32.0
+SQRT_HALF = 0.7071067811865476
+INV_SQRT_TWO_PI = 0.3989422804014327
+
+DP = 8
+REP = 4
+CHUNK = 256
+
+
+def nt_dot(left, right):
+    return lax.dot_general(left, right, (((1,), (1,)), ((), ())), preferred_element_type=F32)
+
+
+def tn_dot(left, right):
+    return lax.dot_general(left, right, (((0,), (0,)), ((), ())), preferred_element_type=F32)
+
+
+def nn_dot(left, right):
+    return jnp.dot(left, right, preferred_element_type=F32)
+
+
+def normalized(values):
+    centre = values - jnp.mean(values, axis=-1, keepdims=True)
+    scale = lax.rsqrt(jnp.mean(centre * centre, axis=-1, keepdims=True) + eps_norm)
+    return centre * scale, scale
+
+
+def gelu_and_slope(values):
+    bell = jnp.exp(values * values * -0.5)
+    t = 1.0 / (1.0 + (0.3275911 * SQRT_HALF) * jnp.abs(values))
+    poly = t * (0.127414796 + t * (-0.142248368 + t * (0.7107068705 + t * (-0.7265760135 + t * 0.5307027145))))
+    tail = poly * bell
+    cdf = jnp.where(values >= 0.0, 1.0 - tail, tail)
+    return values * cdf, cdf + values * (bell * INV_SQRT_TWO_PI)
+
+
+S_TOK, S_POS, S_A, S_AX, S_B, S_BX, S_G, S_GX = 0, 1, 2, 18, 19, 35, 36, 52
+S_HT, S_GB, S_TG = 53, 65, 73
+S_Y = 74
+
+
+def layer_kernel(
+    tokens, positions, missing, wqkv_h, wout_h, wup_h, wdown_h, gains,
+    grad_out, down_out, token_out, gain_out, loss_out,
+    wqkv, wout, wup, wdown, tok, posb, h_one, proj, probs, att, resid, h_two, slope,
+    asum, rsum, pool, msg_a, recv_a, msg_b, send_b, recv_b, recv_b2, units, downs, downs_lo, ga, gp_own,
+    h_t, ht, gbuf, gatt, gh, gacc, recv_g, gx_send, gx_recv, as_mat, down_stage,
+    ysend, keep, yrecv, ring_a, ring_b,
+    load_sem, out_sem, ss, rs,
+):
+    width = h_one.shape[1]
+    hidden = wup.shape[1]
+    rows = h_one.shape[0]
+    half = rows // 2
+    patches = half // 2
+    pairs = HEADS // 2
+    lanes = 128
+    pieces = width // lanes
+    items = missing.shape[1]
+    n_wide = hidden // width
+    n_blocks = n_wide + 4
+    per_block = width // CHUNK
+    n_chunks = n_blocks * per_block
+    score_scale = (width // HEADS) ** -0.5
+
+    S_OI, S_II, S_IO, S_X = (S_Y + n_chunks * n for n in range(1, 5))
+
+    dp = lax.axis_index("dp")
+    z = lax.axis_index("rep")
+    c = dp % 2
+    x = (dp // 2) % 2
+    y = dp // 4
+    yz = y * 4 + z
+
+    def at(yy, xx, cc, zz):
+        return (yy * 4 + xx * 2 + cc, zz)
+
+    core_dev = at(y, x, 1 - c, z)
+    x_dev = at(y, 1 - x, c, z)
+    y_dev = at(1 - y, x, c, z)
+    inner = jnp.logical_and(z >= 1, z <= 2)
+    outer = jnp.logical_not(inner)
+    high = z // 2
+    inner_peer = at(y, x, c, 3 - z)
+    outer_peer = at(y, x, c, 3 * high)
+    inward_peer = at(y, x, c, 1 + high)
+
+    def others():
+        for k in range(1, 16):
+            yield k, y ^ (k & 1), x ^ ((k >> 1) & 1), (z + (k >> 2)) % 4
+
+    def rc(src, dst, idx, dev):
+        return pltpu.make_async_remote_copy(
+            src_ref=src, dst_ref=dst, send_sem=ss.at[idx], recv_sem=rs.at[idx],
+            device_id=dev, device_id_type=MESH,
+        )
+
+    def own_rows(xx):
+        return pl.ds(pl.multiple_of(xx * half, half), half)
+
+    tok_load = pltpu.make_async_copy(tokens.at[x], tok.at[own_rows(x)], load_sem.at[4])
+    tok_load.start()
+    loads = []
+    for n, (src, dst) in enumerate(((wqkv_h, wqkv), (wout_h, wout), (wup_h, wup), (wdown_h, wdown))):
+        loads.append(pltpu.make_async_copy(src.at[x], dst, load_sem.at[n]))
+        loads[-1].start()
+    barrier = pltpu.get_barrier_semaphore()
+    for k, yy, xx, zz in others():
+        pl.semaphore_signal(barrier, inc=1, device_id=at(yy, xx, c, zz), device_id_type=MESH)
+    pl.semaphore_signal(barrier, inc=1, device_id=core_dev, device_id_type=MESH)
+
+    cells = positions[...].astype(F32)
+    cell_rows = jnp.floor((cells + 0.5) * (1.0 / GRID_W))
+    cell_cols = cells - GRID_W * cell_rows
+    posb[x] = jnp.zeros((8, lanes), F32)
+    posb[x, 0:2, 0:patches] = cell_rows
+    posb[x, 2:4, 0:patches] = cell_cols
+    asum[...] = jnp.zeros_like(asum)
+    rsum[...] = jnp.zeros_like(rsum)
+    pool[...] = jnp.zeros_like(pool)
+    gacc[...] = jnp.zeros_like(gacc)
+    msg_b[...] = jnp.zeros_like(msg_b)
+
+    pl.semaphore_wait(barrier, 16)
+    tok_send = rc(tokens.at[1 - x], tok.at[own_rows(x)], S_TOK, x_dev)
+    pos_send = rc(posb.at[x], posb.at[x], S_POS, x_dev)
+    tok_send.start()
+    pos_send.start()
+    tok_load.wait()
+
+    low_lanes = lax.broadcasted_iota(jnp.int32, (patches, lanes), 1) < lanes // 2
+    mask_low = low_lanes.astype(F32).astype(BF16)
+    mask_high = (1.0 - low_lanes.astype(F32)).astype(BF16)
+
+    def two_heads(values):
+        return jnp.concatenate([values * mask_low, values * mask_high], axis=0)
+
+    def fold_heads(values):
+        return jnp.where(low_lanes, values[:patches], values[patches:])
+
+    def img_rows(i):
+        return pl.ds(pl.multiple_of(i * patches, patches), patches)
+
+    gain_one = gains[x, 0:1, :]
+    gain_two = gains[x, 1:2, :]
+
+    loads[0].wait()
+
+    def forward_half(step, carry):
+        xx = x + step - 2 * x * step
+        where = own_rows(xx)
+
+        @pl.when(step == 1)
+        def _():
+            tok_send.wait_recv()
+            pos_send.wait_recv()
+
+        for j in range(2):
+            r = img_rows(xx * 2 + j)
+            n, _ = normalized(tok[r, :].astype(F32))
+            h_one[r, :] = (n * gain_one).astype(BF16)
+        lhs = h_one[where, :]
+        for n in range(3):
+            cols = slice(n * width, (n + 1) * width)
+            proj[where, cols] = nn_dot(lhs, wqkv[:, cols]).astype(BF16)
+
+        def image(j, carry):
+            i = xx * 2 + j
+            r = img_rows(i)
+            cr = jnp.broadcast_to(posb[xx, pl.ds(j, 1), :], (lanes, lanes))
+            cc = jnp.broadcast_to(posb[xx, pl.ds(j + 2, 1), :], (lanes, lanes))
+            row_gap = cr.T - cr
+            col_gap = cc.T - cc
+            dist = jnp.sqrt(row_gap * row_gap + col_gap * col_gap)[:patches, :patches]
+            for p in range(pairs):
+                q = two_heads(proj[r, p * lanes : (p + 1) * lanes])
+                k = proj[r, width + p * lanes : width + (p + 1) * lanes]
+                v = proj[r, 2 * width + p * lanes : 2 * width + (p + 1) * lanes]
+                slopes = [2.0 ** (-8.0 * (2 * p + h + 1) / HEADS) for h in range(2)]
+                alibi = jnp.concatenate([dist * -slopes[0], dist * -slopes[1]], axis=0)
+                s = nt_dot(q, k) * score_scale + alibi
+                e = jnp.exp(s - jnp.max(s, axis=-1, keepdims=True))
+                prob = e * (1.0 / jnp.sum(e, axis=-1, keepdims=True))
+                probs[i * pairs + p] = prob
+                att[r, p * lanes : (p + 1) * lanes] = fold_heads(nn_dot(prob.astype(BF16), v)).astype(BF16)
+            return carry
+
+        lax.fori_loop(0, 2, image, 0)
+        return carry
+
+    lax.fori_loop(0, 2, forward_half, 0)
+
+    loads[1].wait()
+    resid[...] = tok[...].astype(F32) + nn_dot(att[...], wout[...])
+    for i in range(4):
+        r = slice(i * patches, (i + 1) * patches)
+        v = resid[r, :]
+        rsum[i : i + 1, :] = jnp.sum(v, axis=0, keepdims=True)
+        n, _ = normalized(v)
+        h_two[r, :] = (n * gain_two).astype(BF16)
+    loads[2].wait()
+    loads[3].wait()
+
+    def feed(j, carry):
+        cols = pl.ds(pl.multiple_of(j * width, width), width)
+        pre = nn_dot(h_two[...], wup[:, cols])
+        for i in range(4):
+            r = slice(i * patches, (i + 1) * patches)
+            act, slp = gelu_and_slope(pre[r])
+            slope[r, cols] = slp.astype(BF16)
+            asum[i : i + 1, cols] = jnp.sum(act.astype(BF16).astype(F32), axis=0, keepdims=True)
+        a = asum[:, cols]
+        a_high = a.astype(BF16).astype(F32)
+        both = jnp.concatenate([a_high, a - a_high], axis=0).astype(BF16)
+        pool[...] += nn_dot(both, wdown[cols, :])
+        return carry
+
+    lax.fori_loop(0, n_wide, feed, 0)
+
+    pooled = rsum[...] + pool[0:8, :] + pool[8:16, :]
+    s_own = lax.rsqrt(jnp.sum(pooled * pooled, axis=1, keepdims=True) + eps_norm)
+    unit = pooled * s_own
+    for q in range(pieces):
+        msg_a[4 * q : 4 * q + 4, :] = unit[0:4, q * lanes : (q + 1) * lanes]
+    s_high = s_own.astype(BF16).astype(F32)
+    msg_a[24:28, :] = jnp.broadcast_to(s_high[0:4], (4, lanes))
+    msg_a[28:32, :] = jnp.broadcast_to((s_own - s_high)[0:4], (4, lanes))
+    recv_a[c, x, yz] = msg_a[...].astype(BF16)
+    a_copies = []
+    for k, yy, xx, zz in others():
+        a_copies.append(rc(recv_a.at[c, x, yz], recv_a.at[c, x, yz], S_A + k, at(yy, xx, c, zz)))
+        a_copies[-1].start()
+
+    for block in range(DP):
+        for q in range(3):
+            lo = block * 3 * lanes + q * lanes
+            msg_b[block, 4 * q : 4 * q + 4, :] = asum[0:4, lo : lo + lanes]
+    for block in range(DP):
+        send_b[block // 2, block % 2] = msg_b[block].astype(BF16)
+    recv_b[x, yz] = send_b[y * 2 + x]
+    b_copies = []
+    for k, yy, xx, zz in others():
+        b_copies.append(rc(send_b.at[yy * 2 + xx], recv_b.at[x, yz], S_B + k, at(yy, xx, c, zz)))
+        b_copies[-1].start()
+
+    ht_copies = []
+    for w, src in enumerate((h_two, att, h_one)):
+        h_t[w] = src[...].T
+        for rel in range(2):
+            yy = y if rel == 1 else 1 - y
+            for xx in range(2):
+                base = yy * (width // 2) + xx * (width // 4)
+                mine = pl.ds(pl.multiple_of(base + c * (width // 8), width // 8), width // 8)
+                theirs = pl.ds(pl.multiple_of(base + (1 - c) * (width // 8), width // 8), width // 8)
+                lo = (rel * 2 + xx) * (width // 8)
+                ht[w, lo : lo + width // 8, 0:rows] = h_t[w, mine, :]
+                ht_copies.append(
+                    rc(
+                        h_t.at[w, theirs, :],
+                        ht.at[w, pl.ds(lo, width // 8), pl.ds(rows, rows)],
+                        S_HT + w * 4 + rel * 2 + xx,
+                        core_dev,
+                    )
+                )
+                ht_copies[-1].start()
+
+    n_sel = 8 * 32
+    sel_row = lax.broadcasted_iota(jnp.int32, (n_sel, n_sel), 0)
+    sel_col = lax.broadcasted_iota(jnp.int32, (n_sel, n_sel), 1)
+    pick = ((sel_row >> 2) & 7) * 32 + (sel_row >> 5) * 4 + (sel_row & 3)
+    select_a = (sel_col == pick).astype(F32).astype(BF16)
+
+    p_i = lax.broadcasted_iota(jnp.int32, (items, items), 0)
+    q_i = lax.broadcasted_iota(jnp.int32, (items, items), 1)
+    place = ((((p_i >> 4) & 1) * 4 + ((p_i >> 1) & 1) * 2 + (p_i >> 5)) * 4 + ((p_i >> 2) & 3)) * 2 + (p_i & 1)
+    eye = (p_i == q_i).astype(F32)
+    v_nat = 1.0 - missing[...].astype(F32)
+    v_col = jnp.sum((q_i == place).astype(F32) * v_nat, axis=1, keepdims=True)
+    v_row = jnp.sum(eye * v_col, axis=0, keepdims=True)
+
+    for cp in a_copies:
+        cp.wait_recv()
+    ax_copy = rc(recv_a.at[c], recv_a.at[c], S_AX, core_dev)
+    ax_copy.start()
+    ax_copy.wait_recv()
+
+    scales = [[None, None], [None, None]]
+    for core in range(2):
+        for m in range(2):
+            got = nn_dot(select_a, recv_a[core, m].reshape(n_sel, lanes))
+            for q in range(pieces):
+                units[m, core * 32 : core * 32 + 32, q * lanes : (q + 1) * lanes] = got[q * 32 : q * 32 + 32].astype(BF16)
+            scales[m][core] = got[6 * 32 : 7 * 32] + got[7 * 32 :]
+    scale_cols = [jnp.concatenate(scales[m], axis=0)[:, 0:1] for m in range(2)]
+
+    u_r, u_o = units[0], units[1]
+    logits = nt_dot(u_r, u_o) * inv_temp
+    top_r = jnp.max(logits, axis=1, keepdims=True)
+    lse_r = top_r + jnp.log(jnp.sum(v_row * jnp.exp(logits - top_r), axis=1, keepdims=True) + (1.0 - v_col))
+    top_o = jnp.max(logits, axis=0, keepdims=True)
+    lse_o = top_o + jnp.log(jnp.sum(v_col * jnp.exp(logits - top_o), axis=0, keepdims=True) + (1.0 - v_row))
+    diag = logits * eye
+    terms_r = v_col * (lse_r - jnp.sum(diag, axis=1, keepdims=True))
+    terms_o = v_row * (lse_o - jnp.sum(diag, axis=0, keepdims=True))
+    loss = (jnp.sum(terms_r, axis=0, keepdims=True) + jnp.sum(terms_o, axis=1, keepdims=True)) / (2.0 * items)
+    loss_out[...] = jnp.broadcast_to(loss, loss_out.shape)
+    grad_r = (v_col / (2.0 * items) * (v_row * jnp.exp(logits - lse_r) - eye)).astype(BF16)
+    grad_ot = (v_row / (2.0 * items) * (v_col * jnp.exp(logits - lse_o) - eye)).astype(BF16)
+    grad_u = [
+        (nn_dot(grad_r, u_o) + nn_dot(grad_ot, u_o)) * inv_temp,
+        (tn_dot(grad_r, u_r) + tn_dot(grad_ot, u_r)) * inv_temp,
+    ]
+    for m in range(2):
+        u = units[m].astype(F32)
+        g = grad_u[m]
+        gp = scale_cols[m] * (g - u * jnp.sum(u * g, axis=1, keepdims=True))
+        high_part = gp.astype(BF16)
+        downs[m] = high_part
+        downs_lo[m] = (gp - high_part.astype(F32)).astype(BF16)
+    own_r = lax.broadcasted_iota(jnp.int32, (16, items), 0)
+    own_c = lax.broadcasted_iota(jnp.int32, (16, items), 1)
+    mine = jnp.logical_and(own_r < 4, own_c == c * 32 + yz * 4 + own_r).astype(F32).astype(BF16)
+    down_own = nn_dot(mine, downs[x])
+    gp_own[...] = (down_own + nn_dot(mine, downs_lo[x]))[0:8]
+    down_own = down_own.astype(BF16)
+
+    def y_copy(k):
+        return rc(ysend.at[k], yrecv.at[k], S_Y + k, y_dev)
+
+    def oi_copy(k):
+        return rc(keep.at[k], ring_a.at[k], S_OI + k, inward_peer)
+
+    def ii_copy(k):
+        return rc(ring_a.at[k], ring_b.at[k], S_II + k, inner_peer)
+
+    def io_copy(k):
+        return rc(ring_b.at[k], ring_a.at[k], S_IO + k, outer_peer)
+
+    def out_cols(k):
+        return pl.ds(pl.multiple_of(k * CHUNK, CHUNK), CHUNK)
+
+    quarter = width // 8
+
+    def x_copy(k):
+        return rc(
+            yrecv.at[k, pl.ds(pl.multiple_of((1 - x) * quarter, quarter), quarter), :],
+            grad_out.at[x, :, out_cols(k)], S_X + k, x_dev,
+        )
+
+    def here_copy(k):
+        return pltpu.make_async_copy(
+            yrecv.at[k, pl.ds(pl.multiple_of(x * quarter, quarter), quarter), :],
+            grad_out.at[x, :, out_cols(k)], out_sem.at[k],
+        )
+
+    def step_y(k):
+        y_copy(k).wait_recv()
+        keep[k] = (keep[k].astype(F32) + yrecv[k].astype(F32)).astype(BF16)
+
+        @pl.when(outer)
+        def _():
+            oi_copy(k).start()
+
+    def step_a(k):
+        @pl.when(inner)
+        def _():
+            oi_copy(k).wait_recv()
+            ring_a[k] = (ring_a[k].astype(F32) + keep[k].astype(F32)).astype(BF16)
+            ii_copy(k).start()
+
+    def step_b(k):
+        @pl.when(inner)
+        def _():
+            ii_copy(k).wait_recv()
+            got = ring_b[k].astype(F32)
+            ring_b[k] = (got + keep[k].astype(F32)).astype(BF16)
+            io_copy(k).start()
+            yrecv[k] = (got + ring_a[k].astype(F32)).astype(BF16)
+            x_copy(k).start()
+            here_copy(k).start()
+
+    def step_c(k):
+        @pl.when(outer)
+        def _():
+            io_copy(k).wait_recv()
+            yrecv[k] = (keep[k].astype(F32) + ring_a[k].astype(F32)).astype(BF16)
+            x_copy(k).start()
+            here_copy(k).start()
+
+    def comm(t):
+        for lag, step in ((0, step_y), (1, step_a), (2, step_b), (3, step_c)):
+            @pl.when(jnp.logical_and(t >= lag, t < n_chunks + lag))
+            def _(step=step, lag=lag):
+                step(t - lag)
+
+    def gb_copy(j):
+        return rc(gbuf.at[j, pl.ds(0, rows), :], gbuf.at[j, pl.ds(rows, rows), :], S_GB + j, core_dev)
+
+    def wgrad(j, w):
+        gb_copy(j).wait_recv()
+        for n in range(per_block):
+            both = nn_dot(ht[w], gbuf[j, :, n * CHUNK : (n + 1) * CHUNK])
+            k = j * per_block + n
+            ysend[k] = both[:half].astype(BF16)
+            y_copy(k).start()
+            keep[k] = both[half:].astype(BF16)
+
+    for cp in ht_copies[:4]:
+        cp.wait_recv()
+
+    def back_hidden(j, carry):
+        cols = pl.ds(pl.multiple_of(j * width, width), width)
+        ga[...] = nt_dot(down_own, wdown[cols, :])
+        for i in range(4):
+            r = slice(i * patches, (i + 1) * patches)
+            gbuf[j, r, :] = (ga[i : i + 1, :] * slope[r, cols].astype(F32)).astype(BF16)
+        gb_copy(j).start()
+
+        @pl.when(j > 0)
+        def _():
+            wgrad(j - 1, 0)
+
+        return carry
+
+    lax.fori_loop(0, n_wide, back_hidden, 0)
+    wgrad(n_wide - 1, 0)
+
+    gh[...] = jnp.zeros_like(gh)
+
+    def back_up(j, carry):
+        cols = pl.ds(pl.multiple_of(j * width, width), width)
+        gh[...] += nt_dot(gbuf[j, 0:rows, :], wup[:, cols])
+        comm(j)
+        return carry
+
+    lax.fori_loop(0, n_wide, back_up, 0)
+    comm(4)
+
+    for i in range(4):
+        r = slice(i * patches, (i + 1) * patches)
+        n, s = normalized(resid[r, :])
+        gy = gh[r, :]
+        gacc[1:2, :] += jnp.sum(gy * n, axis=0, keepdims=True)
+        gyg = gy * gain_two
+        grad = s * (gyg - jnp.mean(gyg, axis=-1, keepdims=True) - n * jnp.mean(gyg * n, axis=-1, keepdims=True))
+        grad = grad + gp_own[i : i + 1, :]
+        resid[r, :] = grad
+        gbuf[n_wide, r, :] = grad.astype(BF16)
+    gb_copy(n_wide).start()
+    comm(5)
+    gatt[...] = nt_dot(gbuf[n_wide, 0:rows, :], wout[...]).astype(BF16)
+    for cp in ht_copies[4:8]:
+        cp.wait_recv()
+    wgrad(n_wide, 1)
+    comm(6)
+
+    def back_attention(i, carry):
+        r = img_rows(i)
+        for p in range(pairs):
+            cols = slice(p * lanes, (p + 1) * lanes)
+            q = two_heads(proj[r, cols])
+            k = proj[r, width + p * lanes : width + (p + 1) * lanes]
+            v = proj[r, 2 * width + p * lanes : 2 * width + (p + 1) * lanes]
+            da = two_heads(gatt[r, cols])
+            prob = probs[i * pairs + p]
+            dprob = nt_dot(da, v)
+            ds = prob * (dprob - jnp.sum(dprob * prob, axis=-1, keepdims=True))
+            ds = ds.astype(BF16)
+            gbuf[n_wide + 3, r, cols] = tn_dot(prob.astype(BF16), da).astype(BF16)
+            gbuf[n_wide + 1, r, cols] = (fold_heads(nn_dot(ds, k)) * score_scale).astype(BF16)
+            gbuf[n_wide + 2, r, cols] = (tn_dot(ds, q) * score_scale).astype(BF16)
+        comm(7 + i)
+        return carry
+
+    lax.fori_loop(0, 4, back_attention, 0)
+    for n in range(3):
+        gb_copy(n_wide + 1 + n).start()
+    gh[...] = jnp.zeros_like(gh)
+
+    def back_proj(n, carry):
+        cols = pl.ds(pl.multiple_of(n * width, width), width)
+        gh[...] += nt_dot(gbuf[n_wide + 1 + n, 0:rows, :], wqkv[:, cols])
+        comm(11 + n)
+        return carry
+
+    for cp in ht_copies[8:12]:
+        cp.wait_recv()
+    wgrad(n_wide + 1, 2)
+    lax.fori_loop(0, 3, back_proj, 0)
+    wgrad(n_wide + 2, 2)
+    comm(14)
+    wgrad(n_wide + 3, 2)
+    comm(15)
+
+    for i in range(4):
+        r = slice(i * patches, (i + 1) * patches)
+        n, s = normalized(tok[r, :].astype(F32))
+        gy = gh[r, :]
+        gacc[0:1, :] += jnp.sum(gy * n, axis=0, keepdims=True)
+        gyg = gy * gain_one
+        grad = s * (gyg - jnp.mean(gyg, axis=-1, keepdims=True) - n * jnp.mean(gyg * n, axis=-1, keepdims=True))
+        resid[r, :] += grad
+    tg_copy = rc(resid.at[own_rows(1 - x)], token_out.at[x], S_TG, x_dev)
+    tg_copy.start()
+    tg_here = pltpu.make_async_copy(resid.at[own_rows(x)], token_out.at[x], load_sem.at[5])
+    tg_here.start()
+
+    gx_send[...] = jnp.zeros_like(gx_send)
+    for n in range(2):
+        for q in range(pieces):
+            row = n * pieces + q
+            gx_send[0, row : row + 1, :] = gacc[n : n + 1, q * lanes : (q + 1) * lanes]
+    recv_g[x, yz] = gx_send[0]
+    g_copies = []
+    for k, yy, xx, zz in others():
+        g_copies.append(rc(recv_g.at[x, yz], recv_g.at[x, yz], S_G + k, at(yy, xx, c, zz)))
+        g_copies[-1].start()
+    comm(16)
+
+    for cp in b_copies:
+        cp.wait_recv()
+    bx_copy = rc(recv_b.at[:, :, 1 - c], recv_b2, S_BX, core_dev)
+    bx_copy.start()
+    sb_row = lax.broadcasted_iota(jnp.int32, (96, 128), 0)
+    sb_col = lax.broadcasted_iota(jnp.int32, (96, 128), 1)
+    pick_b = ((sb_row >> 2) & 7) * 16 + (sb_row >> 5) * 4 + (sb_row & 3)
+    select_b = (sb_col == pick_b).astype(F32).astype(BF16)
+    comm(17)
+    bx_copy.wait_recv()
+    for m in range(2):
+        for src, cc in ((recv_b[m, :, c], c), (recv_b2[m], 1 - c)):
+            got = nn_dot(select_b, src.reshape(128, lanes)).astype(BF16)
+            to = pl.ds(pl.multiple_of(cc * 32, 32), 32)
+            for q in range(3):
+                as_mat[to, q * lanes : (q + 1) * lanes] = got[q * 32 : (q + 1) * 32]
+        down_stage[m] = tn_dot(as_mat[...], downs[m]).astype(BF16)
+    down_copy = pltpu.make_async_copy(down_stage, down_out, load_sem.at[6])
+    down_copy.start()
+    comm(18)
+
+    for cp in g_copies:
+        cp.wait_recv()
+    for m in range(2):
+        total = recv_g[m, 0]
+        for n in range(1, 8):
+            total = total + recv_g[m, n]
+        gx_send[m] = total
+    gx_copy = rc(gx_send, gx_recv, S_GX, core_dev)
+    gx_copy.start()
+
+    def drain(t, carry):
+        comm(t)
+        return carry
+
+    lax.fori_loop(19, n_chunks + 3, drain, 0)
+    gx_copy.wait_recv()
+    gain_out[...] = gx_send[...] + gx_recv[...]
+
+    def finish(k, carry):
+        y_copy(k).wait_send()
+        here_copy(k).wait()
+        x_copy(k).wait()
+
+        @pl.when(outer)
+        def _():
+            oi_copy(k).wait_send()
+
+        @pl.when(inner)
+        def _():
+            ii_copy(k).wait_send()
+            io_copy(k).wait_send()
+
+        return carry
+
+    lax.fori_loop(0, n_chunks, finish, 0)
+    for cp in a_copies + b_copies + ht_copies + g_copies + [tok_send, pos_send, ax_copy, bx_copy, gx_copy]:
+        cp.wait_send()
+    for j in range(n_blocks):
+        gb_copy(j).wait_send()
+    tg_copy.wait()
+    tg_here.wait()
+    down_copy.wait()
+
+
+def layer_call(tokens, positions, missing, wqkv, wout, wup, wdown, gains):
+    own, patches = positions.shape
+    width = tokens.shape[2]
+    hidden = wup.shape[2]
+    rows = 2 * own * patches
+    items = missing.shape[0]
+    n_blocks = hidden // width + 4
+    n_chunks = n_blocks * (width // CHUNK)
+    piece = (n_chunks, width // 4, CHUNK)
+    vm = pltpu.VMEM
+    any_spec = pl.BlockSpec(memory_space=pl.ANY)
+    vmem_spec = pl.BlockSpec(memory_space=pltpu.VMEM)
+    n_sems = S_Y + 5 * n_chunks
+    scratch = [
+        vm((width, 3 * width), BF16), vm((width, width), BF16), vm((width, hidden), BF16), vm((hidden, width), BF16),
+        vm((rows, width), BF16),
+        vm((2, 8, 128), F32),
+        vm((rows, width), BF16),
+        vm((rows, 3 * width), BF16),
+        vm((4 * (HEADS // 2), 2 * patches, patches), F32),
+        vm((rows, width), BF16),
+        vm((rows, width), F32),
+        vm((rows, width), BF16),
+        vm((rows, hidden), BF16),
+        vm((8, hidden), F32),
+        vm((8, width), F32),
+        vm((16, width), F32),
+        vm((32, 128), F32),
+        vm((2, 2, 8, 32, 128), BF16),
+        vm((8, 16, 128), F32),
+        vm((4, 2, 16, 128), BF16),
+        vm((2, 8, 2, 16, 128), BF16),
+        vm((2, 8, 16, 128), BF16),
+        vm((2, items, width), BF16),
+        vm((2, items, width), BF16),
+        vm((2, items, width), BF16),
+        vm((16, width), F32),
+        vm((8, width), F32),
+        vm((3, width, rows), BF16),
+        vm((3, width // 2, 2 * rows), BF16),
+        vm((n_blocks, 2 * rows, width), BF16),
+        vm((rows, width), BF16),
+        vm((rows, width), F32),
+        vm((8, width), F32),
+        vm((2, 8, 16, 128), F32),
+        vm((2, 16, 128), F32),
+        vm((2, 16, 128), F32),
+        vm((items, hidden // DP), BF16),
+        vm((2, hidden // DP, width), BF16),
+        vm(piece, BF16), vm(piece, BF16), vm(piece, BF16), vm(piece, BF16), vm(piece, BF16),
+        pltpu.SemaphoreType.DMA((8,)),
+        pltpu.SemaphoreType.DMA((n_chunks,)),
+        pltpu.SemaphoreType.DMA((n_sems,)),
+        pltpu.SemaphoreType.DMA((n_sems,)),
+    ]
+    return pl.pallas_call(
+        layer_kernel,
+        out_shape=(
+            jax.ShapeDtypeStruct((2, width // DP, n_chunks * CHUNK), BF16),
+            jax.ShapeDtypeStruct((2, hidden // DP, width), BF16),
+            jax.ShapeDtypeStruct((2, own * patches, width), F32),
+            jax.ShapeDtypeStruct((2, 16, 128), F32),
+            jax.ShapeDtypeStruct((8, 128), F32),
+        ),
+        in_specs=[any_spec, vmem_spec, vmem_spec, any_spec, any_spec, any_spec, any_spec, vmem_spec],
+        out_specs=(any_spec, any_spec, any_spec, vmem_spec, vmem_spec),
+        scratch_shapes=scratch,
+        compiler_params=pltpu.CompilerParams(
+            collective_id=0, has_side_effects=True, vmem_limit_bytes=62 * 2**20
+        ),
+    )(tokens, positions, missing.reshape(1, items), wqkv, wout, wup, wdown, gains)
+
+
+def fused(tokens, positions, missing, qkv_weight, out_weight, up_weight, down_weight, norm_gains):
+    width = tokens.shape[2]
+    hidden = up_weight.shape[2]
+    grads, down, token_grads, gain, loss = layer_call(
+        tokens, positions, missing, qkv_weight, out_weight, up_weight, down_weight, norm_gains
+    )
+    gain = gain[:, : 2 * width // 128].reshape(2, 2, width)
+    share = width // DP
+    gain = lax.dynamic_slice_in_dim(gain, lax.axis_index("dp") * share, share, axis=2)
+    return (
+        loss[0, 0],
+        token_grads,
+        grads[:, :, hidden + width :].astype(F32),
+        grads[:, :, hidden : hidden + width].astype(F32),
+        grads[:, :, :hidden].astype(F32),
+        down.astype(F32),
+        gain,
+    )
 
 
 def lead_dot(left, right):
@@ -280,4 +960,6 @@
         P(None, "dp", None),
         P(None, None, "dp"),
     )
-    return jax.shard_map(local, mesh=mesh, in_specs=in_specs, out_specs=out_specs, check_vma=False)
+    one_kernel = mesh.shape["dp"] == DP and mesh.shape["rep"] == REP
+    step = fused if one_kernel else local
+    return jax.shard_map(step, mesh=mesh, in_specs=in_specs, out_specs=out_specs, check_vma=False)

time: 969 us -> 156 us (0.16)
  waiting for transfers between devices: 555 us -> 0 us
  blocking collectives: 186 us -> 0 us
  Pallas kernels: 0 us -> 143 us
  matrix products: 99.2 us -> 0 us
  other arithmetic: 57.7 us -> 7.54 us
  local copies, waits for them, and re-layouts: 42.4 us -> 3.84 us
  between operations: 18 us -> 0.67 us
    reduce_scatter x4 -> x0, waiting for transfers between devices: 312 us -> none  [the longest x1 127 us: local(): lax.psum_scatter(stacked[2], 'dp', scatter_dimension=1, tiled=True)]
    pallas_call x0 -> x1, Pallas kernels: none -> 143 us  [layer_call(): pl.pallas_call(layer_kernel, out_shape=(jax.ShapeDtypeStruct((2, width //...]
    all_gather x2 -> x0, blocking collectives: 135 us -> none  [the longest x1 70.6 us: local(): lax.all_gather(normed[0], ('dp', 'rep'), axis=0, tiled=True)]
    unnamed x9 -> x0, waiting for transfers between devices: 126 us -> none
    psum x1 -> x0, waiting for transfers between devices: 118 us -> none  [local(): lax.psum(shares[0].astype(jnp.bfloat16), 'rep').astype(jnp.float32)]
    dot_general x40 -> x0, matrix products: 95.9 us -> none  [the longest x10 30 us: tail_dot(): lax.dot_general(left, right, (((1,), (1,)), ((), ())), preferred_element_...]
    psum x2 -> x0, blocking collectives: 51.2 us -> none  [the longest x1 39.6 us: local(): summed_terms = lax.psum(jnp.sum(item_terms), ('dp', 'rep'))]
    another operation x9 -> x0, other arithmetic: 32.7 us -> none  [the longest x7 31.3 us: local(): jnp.stack([block_grads[0][slot], block_grads[1][slot]])]
  transfers between devices with their start and end apart: 7 -> 0, of which waited for: 5 -> 0; matrix products, arithmetic and copies ran while one was open for 12% -> 0% of each run, Pallas kernels for 0% -> 0%
where the time goes in v1:
time: 156 us; the launch traced here: 155 us
  Pallas kernels  143 us (92%)
  other arithmetic  7.54 us (5%)
  local copies, waits for them, and re-layouts  3.84 us (2%)
    pallas_call x1, Pallas kernels, layer_call(): pl.pallas_call(layer_kernel, out_shape=(jax.ShapeDtypeStruct((2, width //...  143 us

profile of v1, /device:TPU:0, one launch (start us, length us, event | category | flops | bytes accessed | tf_op | source)
XLA Modules:
  0.0 155.5 jit_solution(11964425473716106398)
XLA Ops:
  0.6 143.4 %shard_map.135 = (bf16[2,96,6144]{2,1,0:T(8,128)(2,1)}, bf16[2,384,768]{2,1,0:T(8,128)(2,1)}, f32[2,192,768]{2,1,0:T(8,128)}, f32[2,16,128]{2,1,0:T(8,128)}, f32[8,128]{1,0:T(8,128)}) custom-call(bf16[2,192,768]{2,1,0:T(8,128)(2,1)} %tokens.1, s32[2,96]{1,0:T(2,128)} %positions.1, s32[1,64]{1,0:T(1,128)} %bitcast.4, bf16[2,768,2304]{2,1,0:T(8,128)(2,1)} %wqkv_h.1, ...), custom_call_target="tpu_custom_call" | custom-call | tf_op jit(solution)/shard_map/pallas_call | solution.py:656
  144.1 0.0 copy-start
  144.1 1.3 slice.15
  145.4 0.7 reshape.21
  146.2 0.7 constant_dynamic-slice_fusion
  146.8 1.8 %slice_convert_fusion.2 = f32[2,96,768]{2,1,0:T(8,128)} fusion(bf16[2,96,6144]{2,1,0:T(8,128)(2,1)} %get-tuple-element.14), kind=kLoop, calls=%fused_computation.2 | loop fusion | flops 147456 | bytes 884736 | tf_op jit(solution)/shard_map/convert_element_type | solution.py:687
  148.6 2.5 %slice_convert_fusion.1 = f32[2,96,2304]{2,1,0:T(8,128)} fusion(bf16[2,96,6144]{2,1,0:T(8,128)(2,1)} %get-tuple-element.14), kind=kLoop, calls=%fused_computation.1 | loop fusion | flops 442368 | bytes 2654208 | tf_op jit(solution)/shard_map/convert_element_type | solution.py:686
  151.1 0.0 copy-done
  151.1 0.0 copy-start.1
  151.1 1.7 %slice_convert_fusion = f32[2,96,3072]{2,1,0:T(8,128)} fusion(bf16[2,96,6144]{2,1,0:T(8,128)(2,1)S(1)} %copy-done), kind=kLoop, calls=%fused_computation | loop fusion | flops 589824 | bytes 3538944 | tf_op jit(solution)/shard_map/convert_element_type | solution.py:688
  152.8 0.0 copy-done.1
  152.8 0.0 copy-start.2
  152.8 1.6 %convert_element_type.15 = f32[2,384,768]{2,1,0:T(8,128)} convert(bf16[2,384,768]{2,1,0:T(8,128)(2,1)S(1)} %copy-done.1) | non-fusion elementwise | flops 589824 | bytes 3538944 | tf_op jit(solution)/shard_map/convert_element_type | solution.py:689
  154.4 0.1 copy-done.2
  154.5 1.0 copy.16
Async XLA Ops:
  144.1 7.0 %copy-start = (bf16[2,96,6144]{2,1,0:T(8,128)(2,1)S(1)}, bf16[2,96,6144]{2,1,0:T(8,128)(2,1)}, u32[]{:S(2)}) copy-start(bf16[2,96,6144]{2,1,0:T(8,128)(2,1)} %get-tuple-element.14) | copy-start | bytes 7077892
  151.1 1.7 %copy-start.1 = (bf16[2,384,768]{2,1,0:T(8,128)(2,1)S(1)}, bf16[2,384,768]{2,1,0:T(8,128)(2,1)}, u32[]{:S(2)}) copy-start(bf16[2,384,768]{2,1,0:T(8,128)(2,1)} %get-tuple-element.15) | copy-start | bytes 3538948
  152.8 1.7 %copy-start.2 = (f32[2,192,768]{2,1,0:T(8,128)S(1)}, f32[2,192,768]{2,1,0:T(8,128)}, u32[]{:S(2)}) copy-start(f32[2,192,768]{2,1,0:T(8,128)} %get-tuple-element.25) | copy-start | bytes 3538948

commit v2 on v1

--- a/solution.py
+++ b/solution.py
@@ -17,6 +17,7 @@
 inv_temp = 32.0
 SQRT_HALF = 0.7071067811865476
 INV_SQRT_TWO_PI = 0.3989422804014327
+HALF_LOG2_E = -0.7213475204444817
 
 DP = 8
 REP = 4
@@ -42,12 +43,8 @@
 
 
 def gelu_and_slope(values):
-    bell = jnp.exp(values * values * -0.5)
-    t = 1.0 / (1.0 + (0.3275911 * SQRT_HALF) * jnp.abs(values))
-    poly = t * (0.127414796 + t * (-0.142248368 + t * (0.7107068705 + t * (-0.7265760135 + t * 0.5307027145))))
-    tail = poly * bell
-    cdf = jnp.where(values >= 0.0, 1.0 - tail, tail)
-    return values * cdf, cdf + values * (bell * INV_SQRT_TWO_PI)
+    cdf = 0.5 + 0.5 * lax.erf(values * SQRT_HALF)
+    return values * cdf, cdf + values * (jnp.exp2(values * values * HALF_LOG2_E) * INV_SQRT_TWO_PI)
 
 
 S_TOK, S_POS, S_A, S_AX, S_B, S_BX, S_G, S_GX = 0, 1, 2, 18, 19, 35, 36, 52
@@ -56,9 +53,9 @@
 
 
 def layer_kernel(
-    tokens, positions, missing, wqkv_h, wout_h, wup_h, wdown_h, gains,
+    tokens, positions_h, missing_h, wqkv_h, wout_h, wup_h, wdown_h, gains_h,
     grad_out, down_out, token_out, gain_out, loss_out,
-    wqkv, wout, wup, wdown, tok, posb, h_one, proj, probs, att, resid, h_two, slope,
+    positions, missing, gains, gain_stage, loss_stage, wqkv, wout, wup, wdown, tok, posb, h_one, proj, probs, att, resid, h_two, slope,
     asum, rsum, pool, msg_a, recv_a, msg_b, send_b, recv_b, recv_b2, units, downs, downs_lo, ga, gp_own,
     h_t, ht, gbuf, gatt, gh, gacc, recv_g, gx_send, gx_recv, as_mat, down_stage,
     ysend, keep, yrecv, ring_a, ring_b,
@@ -114,35 +111,37 @@
     def own_rows(xx):
         return pl.ds(pl.multiple_of(xx * half, half), half)
 
-    tok_load = pltpu.make_async_copy(tokens.at[x], tok.at[own_rows(x)], load_sem.at[4])
-    tok_load.start()
-    loads = []
-    for n, (src, dst) in enumerate(((wqkv_h, wqkv), (wout_h, wout), (wup_h, wup), (wdown_h, wdown))):
-        loads.append(pltpu.make_async_copy(src.at[x], dst, load_sem.at[n]))
-        loads[-1].start()
     barrier = pltpu.get_barrier_semaphore()
     for k, yy, xx, zz in others():
         pl.semaphore_signal(barrier, inc=1, device_id=at(yy, xx, c, zz), device_id_type=MESH)
     pl.semaphore_signal(barrier, inc=1, device_id=core_dev, device_id_type=MESH)
-
-    cells = positions[...].astype(F32)
-    cell_rows = jnp.floor((cells + 0.5) * (1.0 / GRID_W))
-    cell_cols = cells - GRID_W * cell_rows
+    early = [
+        (positions_h, positions), (tokens.at[x], tok.at[own_rows(x)]), (gains_h.at[x], gains), (wqkv_h.at[x], wqkv),
+        (missing_h, missing),
+    ]
+    late = [(wout_h.at[x], wout), (wup_h.at[x], wup), (wdown_h.at[x], wdown)]
+    loads = [pltpu.make_async_copy(src, dst, load_sem.at[n]) for n, (src, dst) in enumerate(early + late)]
+    for load in loads[: len(early)]:
+        load.start()
+    load_pos, load_tok, load_gains, load_qkv, load_missing, load_out, load_up, load_down = loads
     posb[x] = jnp.zeros((8, lanes), F32)
-    posb[x, 0:2, 0:patches] = cell_rows
-    posb[x, 2:4, 0:patches] = cell_cols
     asum[...] = jnp.zeros_like(asum)
     rsum[...] = jnp.zeros_like(rsum)
     pool[...] = jnp.zeros_like(pool)
     gacc[...] = jnp.zeros_like(gacc)
-    msg_b[...] = jnp.zeros_like(msg_b)
+
+    load_pos.wait()
+    cells = positions[...].astype(F32)
+    cell_rows = jnp.floor((cells + 0.5) * (1.0 / GRID_W))
+    cell_cols = cells - GRID_W * cell_rows
+    posb[x, 0:2, 0:patches] = cell_rows
+    posb[x, 2:4, 0:patches] = cell_cols
 
     pl.semaphore_wait(barrier, 16)
     tok_send = rc(tokens.at[1 - x], tok.at[own_rows(x)], S_TOK, x_dev)
     pos_send = rc(posb.at[x], posb.at[x], S_POS, x_dev)
     tok_send.start()
     pos_send.start()
-    tok_load.wait()
 
     low_lanes = lax.broadcasted_iota(jnp.int32, (patches, lanes), 1) < lanes // 2
     mask_low = low_lanes.astype(F32).astype(BF16)
@@ -157,32 +156,14 @@
     def img_rows(i):
         return pl.ds(pl.multiple_of(i * patches, patches), patches)
 
-    gain_one = gains[x, 0:1, :]
-    gain_two = gains[x, 1:2, :]
-
-    loads[0].wait()
-
-    def forward_half(step, carry):
-        xx = x + step - 2 * x * step
-        where = own_rows(xx)
-
-        @pl.when(step == 1)
-        def _():
-            tok_send.wait_recv()
-            pos_send.wait_recv()
-
-        for j in range(2):
+    load_tok.wait()
+    load_gains.wait()
+    gain_one = gains[0:1, :]
+    gain_two = gains[1:2, :]
+
+    def attention(xx):
+        def image(j, carry):
             r = img_rows(xx * 2 + j)
-            n, _ = normalized(tok[r, :].astype(F32))
-            h_one[r, :] = (n * gain_one).astype(BF16)
-        lhs = h_one[where, :]
-        for n in range(3):
-            cols = slice(n * width, (n + 1) * width)
-            proj[where, cols] = nn_dot(lhs, wqkv[:, cols]).astype(BF16)
-
-        def image(j, carry):
-            i = xx * 2 + j
-            r = img_rows(i)
             cr = jnp.broadcast_to(posb[xx, pl.ds(j, 1), :], (lanes, lanes))
             cc = jnp.broadcast_to(posb[xx, pl.ds(j + 2, 1), :], (lanes, lanes))
             row_gap = cr.T - cr
@@ -197,41 +178,70 @@
                 s = nt_dot(q, k) * score_scale + alibi
                 e = jnp.exp(s - jnp.max(s, axis=-1, keepdims=True))
                 prob = e * (1.0 / jnp.sum(e, axis=-1, keepdims=True))
-                probs[i * pairs + p] = prob
+                probs[(xx * 2 + j) * pairs + p] = prob
                 att[r, p * lanes : (p + 1) * lanes] = fold_heads(nn_dot(prob.astype(BF16), v)).astype(BF16)
             return carry
 
         lax.fori_loop(0, 2, image, 0)
-        return carry
-
-    lax.fori_loop(0, 2, forward_half, 0)
-
-    loads[1].wait()
-    resid[...] = tok[...].astype(F32) + nn_dot(att[...], wout[...])
-    for i in range(4):
-        r = slice(i * patches, (i + 1) * patches)
-        v = resid[r, :]
-        rsum[i : i + 1, :] = jnp.sum(v, axis=0, keepdims=True)
-        n, _ = normalized(v)
-        h_two[r, :] = (n * gain_two).astype(BF16)
-    loads[2].wait()
-    loads[3].wait()
-
-    def feed(j, carry):
-        cols = pl.ds(pl.multiple_of(j * width, width), width)
-        pre = nn_dot(h_two[...], wup[:, cols])
-        for i in range(4):
-            r = slice(i * patches, (i + 1) * patches)
-            act, slp = gelu_and_slope(pre[r])
-            slope[r, cols] = slp.astype(BF16)
-            asum[i : i + 1, cols] = jnp.sum(act.astype(BF16).astype(F32), axis=0, keepdims=True)
-        a = asum[:, cols]
+
+    def wide(j):
+        return pl.ds(pl.multiple_of(j * width, width), width)
+
+    def add_pool(j, on):
+        a = asum[:, wide(j)] * on
         a_high = a.astype(BF16).astype(F32)
         both = jnp.concatenate([a_high, a - a_high], axis=0).astype(BF16)
-        pool[...] += nn_dot(both, wdown[cols, :])
-        return carry
-
-    lax.fori_loop(0, n_wide, feed, 0)
+        pool[...] += nn_dot(both, wdown[wide(j), :])
+
+    for step in range(2):
+        xx = x if step == 0 else 1 - x
+        where = own_rows(xx)
+        if step == 1:
+            tok_send.wait_recv()
+            pos_send.wait_recv()
+        for j in range(2):
+            r = img_rows(xx * 2 + j)
+            n, _ = normalized(tok[r, :].astype(F32))
+            h_one[r, :] = (n * gain_one).astype(BF16)
+        if step == 0:
+            load_qkv.wait()
+            load_out.start()
+            load_up.start()
+            load_down.start()
+        for n in range(3):
+            cols = slice(n * width, (n + 1) * width)
+            proj[where, cols] = nn_dot(h_one[where, :], wqkv[:, cols]).astype(BF16)
+        attention(xx)
+        if step == 0:
+            load_out.wait()
+        resid[where, :] = tok[where, :].astype(F32) + nn_dot(att[where, :], wout[...])
+        for j in range(2):
+            i = xx * 2 + j
+            r = img_rows(i)
+            v = resid[r, :]
+            rsum[pl.ds(i, 1), :] = jnp.sum(v, axis=0, keepdims=True)
+            n, _ = normalized(v)
+            h_two[r, :] = (n * gain_two).astype(BF16)
+        if step == 0:
+            load_up.wait()
+        else:
+            load_down.wait()
+
+        def feed(j, carry, where=where, xx=xx, step=step):
+            for n in range(width // 256):
+                cols = pl.ds(pl.multiple_of(j * width + n * 256, 256), 256)
+                pre = nn_dot(h_two[where, :], wup[:, cols])
+                act, slp = gelu_and_slope(pre)
+                slope[where, cols] = slp.astype(BF16)
+                act = act.astype(BF16).astype(F32)
+                for i in range(2):
+                    asum[pl.ds(xx * 2 + i, 1), cols] = jnp.sum(act[i * patches : (i + 1) * patches], axis=0, keepdims=True)
+            if step == 1:
+                add_pool(jnp.maximum(j - 1, 0), (j > 0).astype(F32))
+            return carry
+
+        lax.fori_loop(0, n_wide, feed, 0)
+    add_pool(n_wide - 1, 1.0)
 
     pooled = rsum[...] + pool[0:8, :] + pool[8:16, :]
     s_own = lax.rsqrt(jnp.sum(pooled * pooled, axis=1, keepdims=True) + eps_norm)
@@ -246,18 +256,6 @@
     for k, yy, xx, zz in others():
         a_copies.append(rc(recv_a.at[c, x, yz], recv_a.at[c, x, yz], S_A + k, at(yy, xx, c, zz)))
         a_copies[-1].start()
-
-    for block in range(DP):
-        for q in range(3):
-            lo = block * 3 * lanes + q * lanes
-            msg_b[block, 4 * q : 4 * q + 4, :] = asum[0:4, lo : lo + lanes]
-    for block in range(DP):
-        send_b[block // 2, block % 2] = msg_b[block].astype(BF16)
-    recv_b[x, yz] = send_b[y * 2 + x]
-    b_copies = []
-    for k, yy, xx, zz in others():
-        b_copies.append(rc(send_b.at[yy * 2 + xx], recv_b.at[x, yz], S_B + k, at(yy, xx, c, zz)))
-        b_copies[-1].start()
 
     ht_copies = []
     for w, src in enumerate((h_two, att, h_one)):
@@ -290,6 +288,7 @@
     q_i = lax.broadcasted_iota(jnp.int32, (items, items), 1)
     place = ((((p_i >> 4) & 1) * 4 + ((p_i >> 1) & 1) * 2 + (p_i >> 5)) * 4 + ((p_i >> 2) & 3)) * 2 + (p_i & 1)
     eye = (p_i == q_i).astype(F32)
+    load_missing.wait()
     v_nat = 1.0 - missing[...].astype(F32)
     v_col = jnp.sum((q_i == place).astype(F32) * v_nat, axis=1, keepdims=True)
     v_row = jnp.sum(eye * v_col, axis=0, keepdims=True)
@@ -319,7 +318,9 @@
     terms_r = v_col * (lse_r - jnp.sum(diag, axis=1, keepdims=True))
     terms_o = v_row * (lse_o - jnp.sum(diag, axis=0, keepdims=True))
     loss = (jnp.sum(terms_r, axis=0, keepdims=True) + jnp.sum(terms_o, axis=1, keepdims=True)) / (2.0 * items)
-    loss_out[...] = jnp.broadcast_to(loss, loss_out.shape)
+    loss_stage[...] = jnp.broadcast_to(loss, loss_stage.shape)
+    loss_copy = pltpu.make_async_copy(loss_stage, loss_out, load_sem.at[8])
+    loss_copy.start()
     grad_r = (v_col / (2.0 * items) * (v_row * jnp.exp(logits - lse_r) - eye)).astype(BF16)
     grad_ot = (v_row / (2.0 * items) * (v_col * jnp.exp(logits - lse_o) - eye)).astype(BF16)
     grad_u = [
@@ -404,7 +405,7 @@
             here_copy(k).start()
 
     def comm(t):
-        for lag, step in ((0, step_y), (1, step_a), (2, step_b), (3, step_c)):
+        for lag, step in ((0, step_y), (2, step_a), (4, step_b), (6, step_c)):
             @pl.when(jnp.logical_and(t >= lag, t < n_chunks + lag))
             def _(step=step, lag=lag):
                 step(t - lag)
@@ -441,16 +442,29 @@
     lax.fori_loop(0, n_wide, back_hidden, 0)
     wgrad(n_wide - 1, 0)
 
+    msg_b[...] = jnp.zeros_like(msg_b)
+    for block in range(DP):
+        for q in range(3):
+            lo = block * 3 * lanes + q * lanes
+            msg_b[block, 4 * q : 4 * q + 4, :] = asum[0:4, lo : lo + lanes]
+    for block in range(DP):
+        send_b[block // 2, block % 2] = msg_b[block].astype(BF16)
+    recv_b[x, yz] = send_b[y * 2 + x]
+    b_copies = []
+    for k, yy, xx, zz in others():
+        b_copies.append(rc(send_b.at[yy * 2 + xx], recv_b.at[x, yz], S_B + k, at(yy, xx, c, zz)))
+        b_copies[-1].start()
+
+
     gh[...] = jnp.zeros_like(gh)
 
     def back_up(j, carry):
         cols = pl.ds(pl.multiple_of(j * width, width), width)
         gh[...] += nt_dot(gbuf[j, 0:rows, :], wup[:, cols])
-        comm(j)
         return carry
 
     lax.fori_loop(0, n_wide, back_up, 0)
-    comm(4)
+    comm(0)
 
     for i in range(4):
         r = slice(i * patches, (i + 1) * patches)
@@ -463,12 +477,12 @@
         resid[r, :] = grad
         gbuf[n_wide, r, :] = grad.astype(BF16)
     gb_copy(n_wide).start()
-    comm(5)
+    comm(1)
     gatt[...] = nt_dot(gbuf[n_wide, 0:rows, :], wout[...]).astype(BF16)
     for cp in ht_copies[4:8]:
         cp.wait_recv()
     wgrad(n_wide, 1)
-    comm(6)
+    comm(2)
 
     def back_attention(i, carry):
         r = img_rows(i)
@@ -485,7 +499,7 @@
             gbuf[n_wide + 3, r, cols] = tn_dot(prob.astype(BF16), da).astype(BF16)
             gbuf[n_wide + 1, r, cols] = (fold_heads(nn_dot(ds, k)) * score_scale).astype(BF16)
             gbuf[n_wide + 2, r, cols] = (tn_dot(ds, q) * score_scale).astype(BF16)
-        comm(7 + i)
+        comm(3 + i)
         return carry
 
     lax.fori_loop(0, 4, back_attention, 0)
@@ -496,17 +510,17 @@
     def back_proj(n, carry):
         cols = pl.ds(pl.multiple_of(n * width, width), width)
         gh[...] += nt_dot(gbuf[n_wide + 1 + n, 0:rows, :], wqkv[:, cols])
-        comm(11 + n)
+        comm(9 + n)
         return carry
 
     for cp in ht_copies[8:12]:
         cp.wait_recv()
     wgrad(n_wide + 1, 2)
+    comm(7)
+    wgrad(n_wide + 2, 2)
+    comm(8)
+    wgrad(n_wide + 3, 2)
     lax.fori_loop(0, 3, back_proj, 0)
-    wgrad(n_wide + 2, 2)
-    comm(14)
-    wgrad(n_wide + 3, 2)
-    comm(15)
 
     for i in range(4):
         r = slice(i * patches, (i + 1) * patches)
@@ -515,10 +529,10 @@
         gacc[0:1, :] += jnp.sum(gy * n, axis=0, keepdims=True)
         gyg = gy * gain_one
         grad = s * (gyg - jnp.mean(gyg, axis=-1, keepdims=True) - n * jnp.mean(gyg * n, axis=-1, keepdims=True))
-        resid[r, :] += grad
-    tg_copy = rc(resid.at[own_rows(1 - x)], token_out.at[x], S_TG, x_dev)
+        tok[r, :] = (resid[r, :] + grad).astype(BF16)
+    tg_copy = rc(tok.at[own_rows(1 - x)], token_out.at[x], S_TG, x_dev)
     tg_copy.start()
-    tg_here = pltpu.make_async_copy(resid.at[own_rows(x)], token_out.at[x], load_sem.at[5])
+    tg_here = pltpu.make_async_copy(tok.at[own_rows(x)], token_out.at[x], load_sem.at[9])
     tg_here.start()
 
     gx_send[...] = jnp.zeros_like(gx_send)
@@ -531,7 +545,7 @@
     for k, yy, xx, zz in others():
         g_copies.append(rc(recv_g.at[x, yz], recv_g.at[x, yz], S_G + k, at(yy, xx, c, zz)))
         g_copies[-1].start()
-    comm(16)
+    comm(12)
 
     for cp in b_copies:
         cp.wait_recv()
@@ -541,7 +555,7 @@
     sb_col = lax.broadcasted_iota(jnp.int32, (96, 128), 1)
     pick_b = ((sb_row >> 2) & 7) * 16 + (sb_row >> 5) * 4 + (sb_row & 3)
     select_b = (sb_col == pick_b).astype(F32).astype(BF16)
-    comm(17)
+    comm(13)
     bx_copy.wait_recv()
     for m in range(2):
         for src, cc in ((recv_b[m, :, c], c), (recv_b2[m], 1 - c)):
@@ -550,9 +564,9 @@
             for q in range(3):
                 as_mat[to, q * lanes : (q + 1) * lanes] = got[q * 32 : (q + 1) * 32]
         down_stage[m] = tn_dot(as_mat[...], downs[m]).astype(BF16)
-    down_copy = pltpu.make_async_copy(down_stage, down_out, load_sem.at[6])
+    down_copy = pltpu.make_async_copy(down_stage, down_out, load_sem.at[10])
     down_copy.start()
-    comm(18)
+    comm(14)
 
     for cp in g_copies:
         cp.wait_recv()
@@ -568,9 +582,21 @@
         comm(t)
         return carry
 
-    lax.fori_loop(19, n_chunks + 3, drain, 0)
+    lax.fori_loop(15, n_chunks + 6, drain, 0)
     gx_copy.wait_recv()
-    gain_out[...] = gx_send[...] + gx_recv[...]
+    total = gx_send[...] + gx_recv[...]
+    for m in range(2):
+        flat = jnp.concatenate(
+            [jnp.concatenate([total[m, n * pieces + q : n * pieces + q + 1] for q in range(pieces)], axis=1) for n in range(2)],
+            axis=0,
+        )
+        share = width // DP
+        own = flat[:, 0:share]
+        for d in range(1, DP):
+            own = jnp.where(dp == d, flat[:, d * share : (d + 1) * share], own)
+        gain_stage[m, 0:2, 0:share] = own
+    gain_copy = pltpu.make_async_copy(gain_stage, gain_out, load_sem.at[11])
+    gain_copy.start()
 
     def finish(k, carry):
         y_copy(k).wait_send()
@@ -596,6 +622,8 @@
     tg_copy.wait()
     tg_here.wait()
     down_copy.wait()
+    loss_copy.wait()
+    gain_copy.wait()
 
 
 def layer_call(tokens, positions, missing, wqkv, wout, wup, wdown, gains):
@@ -609,9 +637,9 @@
     piece = (n_chunks, width // 4, CHUNK)
     vm = pltpu.VMEM
     any_spec = pl.BlockSpec(memory_space=pl.ANY)
-    vmem_spec = pl.BlockSpec(memory_space=pltpu.VMEM)
     n_sems = S_Y + 5 * n_chunks
     scratch = [
+        vm((own, patches), jnp.int32), vm((1, items), jnp.int32), vm((2, width), F32), vm((2, 8, 128), F32), vm((8, 128), F32),
         vm((width, 3 * width), BF16), vm((width, width), BF16), vm((width, hidden), BF16), vm((hidden, width), BF16),
         vm((rows, width), BF16),
         vm((2, 8, 128), F32),
@@ -648,7 +676,7 @@
         vm((items, hidden // DP), BF16),
         vm((2, hidden // DP, width), BF16),
         vm(piece, BF16), vm(piece, BF16), vm(piece, BF16), vm(piece, BF16), vm(piece, BF16),
-        pltpu.SemaphoreType.DMA((8,)),
+        pltpu.SemaphoreType.DMA((12,)),
         pltpu.SemaphoreType.DMA((n_chunks,)),
         pltpu.SemaphoreType.DMA((n_sems,)),
         pltpu.SemaphoreType.DMA((n_sems,)),
@@ -658,12 +686,12 @@
         out_shape=(
             jax.ShapeDtypeStruct((2, width // DP, n_chunks * CHUNK), BF16),
             jax.ShapeDtypeStruct((2, hidden // DP, width), BF16),
-            jax.ShapeDtypeStruct((2, own * patches, width), F32),
-            jax.ShapeDtypeStruct((2, 16, 128), F32),
+            jax.ShapeDtypeStruct((2, own * patches, width), BF16),
+            jax.ShapeDtypeStruct((2, 8, 128), F32),
             jax.ShapeDtypeStruct((8, 128), F32),
         ),
-        in_specs=[any_spec, vmem_spec, vmem_spec, any_spec, any_spec, any_spec, any_spec, vmem_spec],
-        out_specs=(any_spec, any_spec, any_spec, vmem_spec, vmem_spec),
+        in_specs=[any_spec] * 8,
+        out_specs=(any_spec,) * 5,
         scratch_shapes=scratch,
         compiler_params=pltpu.CompilerParams(
             collective_id=0, has_side_effects=True, vmem_limit_bytes=62 * 2**20
@@ -671,24 +699,63 @@
     )(tokens, positions, missing.reshape(1, items), wqkv, wout, wup, wdown, gains)
 
 
+def widen_kernel(
+    grads, down, tok, gain, loss, qkv_o, out_o, up_o, down_o, tok_o, gain_o, loss_o,
+    grads_v, down_v, tok_v, gain_v, loss_v, qkv_v, out_v, up_v, down_w, tok_w, in_sem, out_sem,
+):
+    hidden, width = up_v.shape[2], out_v.shape[2]
+    spans = ((0, hidden, up_v, up_o), (hidden, width, out_v, out_o), (hidden + width, 3 * width, qkv_v, qkv_o))
+    moves = [(loss, loss_v, None, None, None), (gain, gain_v, None, None, None)]
+    for m in range(2):
+        moves.append((tok.at[m], tok_v.at[m], tok_w.at[m], tok_o.at[m], None))
+        moves.append((down.at[m], down_v.at[m], down_w.at[m], down_o.at[m], None))
+        for lo, size, wide_v, wide_o in spans:
+            moves.append(
+                (grads.at[m, :, pl.ds(lo, size)], grads_v.at[m, :, pl.ds(lo, size)], wide_v.at[m], wide_o.at[m], None)
+            )
+    ins = [pltpu.make_async_copy(move[0], move[1], in_sem.at[n]) for n, move in enumerate(moves)]
+    for cp in ins:
+        cp.start()
+    outs = []
+    for n, (_, narrow, wide, dst, _) in enumerate(moves):
+        ins[n].wait()
+        if dst is None:
+            continue
+        wide[...] = narrow[...].astype(F32)
+        outs.append(pltpu.make_async_copy(wide, dst, out_sem.at[n]))
+        outs[-1].start()
+    loss_o[...] = loss_v[0:1, 0:1]
+    gain_o[...] = gain_v[:, 0:2, 0 : gain_o.shape[2]]
+    for cp in outs:
+        cp.wait()
+
+
+def widen_call(grads, down, tok, gain, loss, width, hidden):
+    vm = pltpu.VMEM
+    any_spec = pl.BlockSpec(memory_space=pl.ANY)
+    vmem_spec = pl.BlockSpec(memory_space=pltpu.VMEM)
+    rows = width // DP
+    shapes = ((2, rows, 3 * width), (2, rows, width), (2, rows, hidden), down.shape, tok.shape)
+    return pl.pallas_call(
+        widen_kernel,
+        out_shape=tuple(jax.ShapeDtypeStruct(shape, F32) for shape in shapes + ((2, 2, rows), (1, 1))),
+        in_specs=[any_spec] * 5,
+        out_specs=(any_spec,) * 5 + (vmem_spec,) * 2,
+        scratch_shapes=[vm(v.shape, v.dtype) for v in (grads, down, tok, gain, loss)]
+        + [vm(shape, F32) for shape in shapes]
+        + [pltpu.SemaphoreType.DMA((16,)), pltpu.SemaphoreType.DMA((16,))],
+        compiler_params=pltpu.CompilerParams(vmem_limit_bytes=62 * 2**20),
+    )(grads, down, tok, gain, loss)
+
+
 def fused(tokens, positions, missing, qkv_weight, out_weight, up_weight, down_weight, norm_gains):
-    width = tokens.shape[2]
-    hidden = up_weight.shape[2]
-    grads, down, token_grads, gain, loss = layer_call(
+    grads, down, tok, gain, loss = layer_call(
         tokens, positions, missing, qkv_weight, out_weight, up_weight, down_weight, norm_gains
     )
-    gain = gain[:, : 2 * width // 128].reshape(2, 2, width)
-    share = width // DP
-    gain = lax.dynamic_slice_in_dim(gain, lax.axis_index("dp") * share, share, axis=2)
-    return (
-        loss[0, 0],
-        token_grads,
-        grads[:, :, hidden + width :].astype(F32),
-        grads[:, :, hidden : hidden + width].astype(F32),
-        grads[:, :, :hidden].astype(F32),
-        down.astype(F32),
-        gain,
-    )
+    qkv, out, up, down, tok, gain, loss = widen_call(
+        grads, down, tok, gain, loss, tokens.shape[2], up_weight.shape[2]
+    )
+    return (loss.reshape(()), tok, qkv, out, up, down, gain)
 
 
 def lead_dot(left, right):

time: 156 us -> 127 us (0.81)
  Pallas kernels: 143 us -> 126 us
  other arithmetic: 7.54 us -> 0 us
  local copies, waits for them, and re-layouts: 3.84 us -> 0 us
    pallas_call x1, Pallas kernels: 143 us -> 121 us  [layer_call(): pl.pallas_call(layer_kernel, out_shape=(jax.ShapeDtypeStruct((2, width //...]
    convert_element_type x4 -> x0, other arithmetic: 7.54 us -> none  [the longest x1 2.49 us: fused(): grads[:, :, hidden + width:].astype(F32)]
    pallas_call x0 -> x1, Pallas kernels: none -> 5.18 us  [widen_call(): pl.pallas_call(widen_kernel, out_shape=tuple((jax.ShapeDtypeStruct(shape,...]
where the time goes in v2:
time: 127 us
  Pallas kernels  126 us (99%)
    pallas_call x1, Pallas kernels, layer_call(): pl.pallas_call(layer_kernel, out_shape=(jax.ShapeDtypeStruct((2, width //...  121 us
    pallas_call x1, Pallas kernels, widen_call(): pl.pallas_call(widen_kernel, out_shape=tuple((jax.ShapeDtypeStruct(shape,...  5.18 us

profile of v2, /device:TPU:0, one launch (start us, length us, event | category | flops | bytes accessed | tf_op | source)
XLA Modules:
  0.0 126.8 jit_solution(1195714930011376939)
XLA Ops:
  0.6 120.9 %shard_map.135 = (bf16[2,96,6144]{2,1,0:T(8,128)(2,1)}, bf16[2,384,768]{2,1,0:T(8,128)(2,1)}, bf16[2,192,768]{2,1,0:T(8,128)(2,1)}, f32[2,8,128]{2,1,0:T(8,128)}, f32[8,128]{1,0:T(8,128)}) custom-call(bf16[2,192,768]{2,1,0:T(8,128)(2,1)} %tokens.1, s32[2,96]{1,0:T(2,128)} %positions_h.1, s32[1,64]{1,0:T(1,128)} %bitcast.2, bf16[2,768,2304]{2,1,0:T(8,128)(2,1)} %wqkv_h.1, ...), custom_call_target="tpu_custom_call" | custom-call | tf_op jit(solution)/shard_map/pallas_call | solution.py:684
  121.5 5.2 %shard_map.136 = (f32[2,96,2304]{2,1,0:T(8,128)}, f32[2,96,768]{2,1,0:T(8,128)}, f32[2,96,3072]{2,1,0:T(8,128)}, f32[2,384,768]{2,1,0:T(8,128)}, f32[2,192,768]{...) custom-call(bf16[2,96,6144]{2,1,0:T(8,128)(2,1)} %get-tuple-element.19.grads, ...), custom_call_target="tpu_custom_call" | custom-call | tf_op jit(solution)/shard_map/pallas_call | solution.py:739

commit v3 on v2

--- a/solution.py
+++ b/solution.py
@@ -55,9 +55,9 @@
 def layer_kernel(
     tokens, positions_h, missing_h, wqkv_h, wout_h, wup_h, wdown_h, gains_h,
     grad_out, down_out, token_out, gain_out, loss_out,
-    positions, missing, gains, gain_stage, loss_stage, wqkv, wout, wup, wdown, tok, posb, h_one, proj, probs, att, resid, h_two, slope,
+    positions, missing, gains, wqkv, wout, wup, wdown, tok, posb, h_one, proj, probs, att, resid, h_two, slope,
     asum, rsum, pool, msg_a, recv_a, msg_b, send_b, recv_b, recv_b2, units, downs, downs_lo, ga, gp_own,
-    h_t, ht, gbuf, gatt, gh, gacc, recv_g, gx_send, gx_recv, as_mat, down_stage,
+    h_t, ht, gbuf, gatt, gh, gacc, recv_g, gx_send, gx_recv, as_mat,
     ysend, keep, yrecv, ring_a, ring_b,
     load_sem, out_sem, ss, rs,
 ):
@@ -169,17 +169,22 @@
             row_gap = cr.T - cr
             col_gap = cc.T - cc
             dist = jnp.sqrt(row_gap * row_gap + col_gap * col_gap)[:patches, :patches]
+            raw = []
             for p in range(pairs):
                 q = two_heads(proj[r, p * lanes : (p + 1) * lanes])
-                k = proj[r, width + p * lanes : width + (p + 1) * lanes]
-                v = proj[r, 2 * width + p * lanes : 2 * width + (p + 1) * lanes]
+                raw.append(nt_dot(q, proj[r, width + p * lanes : width + (p + 1) * lanes]))
+            soft = []
+            for p in range(pairs):
                 slopes = [2.0 ** (-8.0 * (2 * p + h + 1) / HEADS) for h in range(2)]
                 alibi = jnp.concatenate([dist * -slopes[0], dist * -slopes[1]], axis=0)
-                s = nt_dot(q, k) * score_scale + alibi
+                s = raw[p] * score_scale + alibi
                 e = jnp.exp(s - jnp.max(s, axis=-1, keepdims=True))
                 prob = e * (1.0 / jnp.sum(e, axis=-1, keepdims=True))
                 probs[(xx * 2 + j) * pairs + p] = prob
-                att[r, p * lanes : (p + 1) * lanes] = fold_heads(nn_dot(prob.astype(BF16), v)).astype(BF16)
+                soft.append(prob.astype(BF16))
+            for p in range(pairs):
+                v = proj[r, 2 * width + p * lanes : 2 * width + (p + 1) * lanes]
+                att[r, p * lanes : (p + 1) * lanes] = fold_heads(nn_dot(soft[p], v)).astype(BF16)
             return carry
 
         lax.fori_loop(0, 2, image, 0)
@@ -257,6 +262,14 @@
         a_copies.append(rc(recv_a.at[c, x, yz], recv_a.at[c, x, yz], S_A + k, at(yy, xx, c, zz)))
         a_copies[-1].start()
 
+    msg_b[...] = jnp.zeros_like(msg_b)
+    for block in range(DP):
+        for q in range(3):
+            lo = block * 3 * lanes + q * lanes
+            msg_b[block, 4 * q : 4 * q + 4, :] = asum[0:4, lo : lo + lanes]
+    for block in range(DP):
+        send_b[block // 2, block % 2] = msg_b[block].astype(BF16)
+    recv_b[x, yz] = send_b[y * 2 + x]
     ht_copies = []
     for w, src in enumerate((h_two, att, h_one)):
         h_t[w] = src[...].T
@@ -297,6 +310,10 @@
         cp.wait_recv()
     ax_copy = rc(recv_a.at[c], recv_a.at[c], S_AX, core_dev)
     ax_copy.start()
+    b_copies = []
+    for k, yy, xx, zz in others():
+        b_copies.append(rc(send_b.at[yy * 2 + xx], recv_b.at[x, yz], S_B + k, at(yy, xx, c, zz)))
+        b_copies[-1].start()
     ax_copy.wait_recv()
 
     scales = [[None, None], [None, None]]
@@ -318,9 +335,7 @@
     terms_r = v_col * (lse_r - jnp.sum(diag, axis=1, keepdims=True))
     terms_o = v_row * (lse_o - jnp.sum(diag, axis=0, keepdims=True))
     loss = (jnp.sum(terms_r, axis=0, keepdims=True) + jnp.sum(terms_o, axis=1, keepdims=True)) / (2.0 * items)
-    loss_stage[...] = jnp.broadcast_to(loss, loss_stage.shape)
-    loss_copy = pltpu.make_async_copy(loss_stage, loss_out, load_sem.at[8])
-    loss_copy.start()
+    loss_out[...] = jnp.broadcast_to(loss, loss_out.shape)
     grad_r = (v_col / (2.0 * items) * (v_row * jnp.exp(logits - lse_r) - eye)).astype(BF16)
     grad_ot = (v_row / (2.0 * items) * (v_col * jnp.exp(logits - lse_o) - eye)).astype(BF16)
     grad_u = [
@@ -441,30 +456,21 @@
 
     lax.fori_loop(0, n_wide, back_hidden, 0)
     wgrad(n_wide - 1, 0)
-
-    msg_b[...] = jnp.zeros_like(msg_b)
-    for block in range(DP):
-        for q in range(3):
-            lo = block * 3 * lanes + q * lanes
-            msg_b[block, 4 * q : 4 * q + 4, :] = asum[0:4, lo : lo + lanes]
-    for block in range(DP):
-        send_b[block // 2, block % 2] = msg_b[block].astype(BF16)
-    recv_b[x, yz] = send_b[y * 2 + x]
-    b_copies = []
-    for k, yy, xx, zz in others():
-        b_copies.append(rc(send_b.at[yy * 2 + xx], recv_b.at[x, yz], S_B + k, at(yy, xx, c, zz)))
-        b_copies[-1].start()
-
+    comm(0)
 
     gh[...] = jnp.zeros_like(gh)
 
     def back_up(j, carry):
         cols = pl.ds(pl.multiple_of(j * width, width), width)
         gh[...] += nt_dot(gbuf[j, 0:rows, :], wup[:, cols])
+
+        @pl.when(j == 2)
+        def _():
+            comm(1)
+
         return carry
 
     lax.fori_loop(0, n_wide, back_up, 0)
-    comm(0)
 
     for i in range(4):
         r = slice(i * patches, (i + 1) * patches)
@@ -477,28 +483,30 @@
         resid[r, :] = grad
         gbuf[n_wide, r, :] = grad.astype(BF16)
     gb_copy(n_wide).start()
-    comm(1)
     gatt[...] = nt_dot(gbuf[n_wide, 0:rows, :], wout[...]).astype(BF16)
+    comm(2)
     for cp in ht_copies[4:8]:
         cp.wait_recv()
     wgrad(n_wide, 1)
-    comm(2)
 
     def back_attention(i, carry):
         r = img_rows(i)
+        das, dps, dss = [], [], []
+        for p in range(pairs):
+            da = two_heads(gatt[r, p * lanes : (p + 1) * lanes])
+            das.append(da)
+            dps.append(nt_dot(da, proj[r, 2 * width + p * lanes : 2 * width + (p + 1) * lanes]))
+        for p in range(pairs):
+            cols = slice(p * lanes, (p + 1) * lanes)
+            prob = probs[i * pairs + p]
+            dss.append((prob * (dps[p] - jnp.sum(dps[p] * prob, axis=-1, keepdims=True))).astype(BF16))
+            gbuf[n_wide + 3, r, cols] = tn_dot(prob.astype(BF16), das[p]).astype(BF16)
         for p in range(pairs):
             cols = slice(p * lanes, (p + 1) * lanes)
             q = two_heads(proj[r, cols])
             k = proj[r, width + p * lanes : width + (p + 1) * lanes]
-            v = proj[r, 2 * width + p * lanes : 2 * width + (p + 1) * lanes]
-            da = two_heads(gatt[r, cols])
-            prob = probs[i * pairs + p]
-            dprob = nt_dot(da, v)
-            ds = prob * (dprob - jnp.sum(dprob * prob, axis=-1, keepdims=True))
-            ds = ds.astype(BF16)
-            gbuf[n_wide + 3, r, cols] = tn_dot(prob.astype(BF16), da).astype(BF16)
-            gbuf[n_wide + 1, r, cols] = (fold_heads(nn_dot(ds, k)) * score_scale).astype(BF16)
-            gbuf[n_wide + 2, r, cols] = (tn_dot(ds, q) * score_scale).astype(BF16)
+            gbuf[n_wide + 1, r, cols] = (fold_heads(nn_dot(dss[p], k)) * score_scale).astype(BF16)
+            gbuf[n_wide + 2, r, cols] = (tn_dot(dss[p], q) * score_scale).astype(BF16)
         comm(3 + i)
         return carry
 
@@ -510,17 +518,10 @@
     def back_proj(n, carry):
         cols = pl.ds(pl.multiple_of(n * width, width), width)
         gh[...] += nt_dot(gbuf[n_wide + 1 + n, 0:rows, :], wqkv[:, cols])
-        comm(9 + n)
         return carry
 
-    for cp in ht_copies[8:12]:
-        cp.wait_recv()
-    wgrad(n_wide + 1, 2)
+    lax.fori_loop(0, 3, back_proj, 0)
     comm(7)
-    wgrad(n_wide + 2, 2)
-    comm(8)
-    wgrad(n_wide + 3, 2)
-    lax.fori_loop(0, 3, back_proj, 0)
 
     for i in range(4):
         r = slice(i * patches, (i + 1) * patches)
@@ -534,6 +535,13 @@
     tg_copy.start()
     tg_here = pltpu.make_async_copy(tok.at[own_rows(x)], token_out.at[x], load_sem.at[9])
     tg_here.start()
+
+    comm(8)
+    for cp in ht_copies[8:12]:
+        cp.wait_recv()
+    for n in range(3):
+        wgrad(n_wide + 1 + n, 2)
+        comm(9 + n)
 
     gx_send[...] = jnp.zeros_like(gx_send)
     for n in range(2):
@@ -563,11 +571,14 @@
             to = pl.ds(pl.multiple_of(cc * 32, 32), 32)
             for q in range(3):
                 as_mat[to, q * lanes : (q + 1) * lanes] = got[q * 32 : (q + 1) * 32]
-        down_stage[m] = tn_dot(as_mat[...], downs[m]).astype(BF16)
-    down_copy = pltpu.make_async_copy(down_stage, down_out, load_sem.at[10])
-    down_copy.start()
+        down_out[m] = tn_dot(as_mat[...], downs[m]).astype(BF16)
     comm(14)
 
+    def drain(t, carry):
+        comm(t)
+        return carry
+
+    lax.fori_loop(15, n_chunks + 3, drain, 0)
     for cp in g_copies:
         cp.wait_recv()
     for m in range(2):
@@ -577,12 +588,7 @@
         gx_send[m] = total
     gx_copy = rc(gx_send, gx_recv, S_GX, core_dev)
     gx_copy.start()
-
-    def drain(t, carry):
-        comm(t)
-        return carry
-
-    lax.fori_loop(15, n_chunks + 6, drain, 0)
+    lax.fori_loop(n_chunks + 3, n_chunks + 6, drain, 0)
     gx_copy.wait_recv()
     total = gx_send[...] + gx_recv[...]
     for m in range(2):
@@ -594,9 +600,7 @@
         own = flat[:, 0:share]
         for d in range(1, DP):
             own = jnp.where(dp == d, flat[:, d * share : (d + 1) * share], own)
-        gain_stage[m, 0:2, 0:share] = own
-    gain_copy = pltpu.make_async_copy(gain_stage, gain_out, load_sem.at[11])
-    gain_copy.start()
+        gain_out[m, 0:2, 0:share] = own
 
     def finish(k, carry):
         y_copy(k).wait_send()
@@ -621,9 +625,6 @@
         gb_copy(j).wait_send()
     tg_copy.wait()
     tg_here.wait()
-    down_copy.wait()
-    loss_copy.wait()
-    gain_copy.wait()
 
 
 def layer_call(tokens, positions, missing, wqkv, wout, wup, wdown, gains):
@@ -639,7 +640,7 @@
     any_spec = pl.BlockSpec(memory_space=pl.ANY)
     n_sems = S_Y + 5 * n_chunks
     scratch = [
-        vm((own, patches), jnp.int32), vm((1, items), jnp.int32), vm((2, width), F32), vm((2, 8, 128), F32), vm((8, 128), F32),
+        vm((own, patches), jnp.int32), vm((1, items), jnp.int32), vm((2, width), F32),
         vm((width, 3 * width), BF16), vm((width, width), BF16), vm((width, hidden), BF16), vm((hidden, width), BF16),
         vm((rows, width), BF16),
         vm((2, 8, 128), F32),
@@ -674,7 +675,6 @@
         vm((2, 16, 128), F32),
         vm((2, 16, 128), F32),
         vm((items, hidden // DP), BF16),
-        vm((2, hidden // DP, width), BF16),
         vm(piece, BF16), vm(piece, BF16), vm(piece, BF16), vm(piece, BF16), vm(piece, BF16),
         pltpu.SemaphoreType.DMA((12,)),
         pltpu.SemaphoreType.DMA((n_chunks,)),
@@ -684,68 +684,56 @@
     return pl.pallas_call(
         layer_kernel,
         out_shape=(
-            jax.ShapeDtypeStruct((2, width // DP, n_chunks * CHUNK), BF16),
-            jax.ShapeDtypeStruct((2, hidden // DP, width), BF16),
-            jax.ShapeDtypeStruct((2, own * patches, width), BF16),
-            jax.ShapeDtypeStruct((2, 8, 128), F32),
-            jax.ShapeDtypeStruct((8, 128), F32),
+            vm((2, width // DP, n_chunks * CHUNK), BF16), vm((2, hidden // DP, width), BF16),
+            vm((2, own * patches, width), BF16), vm((2, 8, 128), F32), vm((8, 128), F32),
         ),
         in_specs=[any_spec] * 8,
-        out_specs=(any_spec,) * 5,
+        out_specs=(pl.BlockSpec(memory_space=pltpu.VMEM),) * 5,
         scratch_shapes=scratch,
         compiler_params=pltpu.CompilerParams(
-            collective_id=0, has_side_effects=True, vmem_limit_bytes=62 * 2**20
+            collective_id=0, has_side_effects=True, vmem_limit_bytes=58 * 2**20
         ),
     )(tokens, positions, missing.reshape(1, items), wqkv, wout, wup, wdown, gains)
 
 
 def widen_kernel(
-    grads, down, tok, gain, loss, qkv_o, out_o, up_o, down_o, tok_o, gain_o, loss_o,
-    grads_v, down_v, tok_v, gain_v, loss_v, qkv_v, out_v, up_v, down_w, tok_w, in_sem, out_sem,
+    grads, down, tok, gain, loss, qkv_o, out_o, up_o, down_o, tok_o, gain_o, loss_o, qkv_v, out_v, up_v, down_v, tok_v, sem
 ):
     hidden, width = up_v.shape[2], out_v.shape[2]
-    spans = ((0, hidden, up_v, up_o), (hidden, width, out_v, out_o), (hidden + width, 3 * width, qkv_v, qkv_o))
-    moves = [(loss, loss_v, None, None, None), (gain, gain_v, None, None, None)]
+    outs = []
+
+    def send(value, wide, dst):
+        wide[...] = value.astype(F32)
+        outs.append(pltpu.make_async_copy(wide, dst, sem.at[len(outs)]))
+        outs[-1].start()
+
     for m in range(2):
-        moves.append((tok.at[m], tok_v.at[m], tok_w.at[m], tok_o.at[m], None))
-        moves.append((down.at[m], down_v.at[m], down_w.at[m], down_o.at[m], None))
-        for lo, size, wide_v, wide_o in spans:
-            moves.append(
-                (grads.at[m, :, pl.ds(lo, size)], grads_v.at[m, :, pl.ds(lo, size)], wide_v.at[m], wide_o.at[m], None)
-            )
-    ins = [pltpu.make_async_copy(move[0], move[1], in_sem.at[n]) for n, move in enumerate(moves)]
-    for cp in ins:
-        cp.start()
-    outs = []
-    for n, (_, narrow, wide, dst, _) in enumerate(moves):
-        ins[n].wait()
-        if dst is None:
-            continue
-        wide[...] = narrow[...].astype(F32)
-        outs.append(pltpu.make_async_copy(wide, dst, out_sem.at[n]))
-        outs[-1].start()
-    loss_o[...] = loss_v[0:1, 0:1]
-    gain_o[...] = gain_v[:, 0:2, 0 : gain_o.shape[2]]
+        send(tok[m], tok_v.at[m], tok_o.at[m])
+        send(down[m], down_v.at[m], down_o.at[m])
+        for lo, size, wide, dst in (
+            (0, hidden, up_v, up_o), (hidden, width, out_v, out_o), (hidden + width, 3 * width, qkv_v, qkv_o)
+        ):
+            send(grads[m, :, lo : lo + size], wide.at[m], dst.at[m])
+    loss_o[...] = loss[0:1, 0:1]
+    gain_o[...] = gain[:, 0:2, 0 : gain_o.shape[2]]
     for cp in outs:
         cp.wait()
 
 
 def widen_call(grads, down, tok, gain, loss, width, hidden):
     vm = pltpu.VMEM
-    any_spec = pl.BlockSpec(memory_space=pl.ANY)
     vmem_spec = pl.BlockSpec(memory_space=pltpu.VMEM)
     rows = width // DP
     shapes = ((2, rows, 3 * width), (2, rows, width), (2, rows, hidden), down.shape, tok.shape)
+    ins = [pltpu.with_memory_space_constraint(v, pltpu.VMEM) for v in (grads, down, tok, gain, loss)]
     return pl.pallas_call(
         widen_kernel,
         out_shape=tuple(jax.ShapeDtypeStruct(shape, F32) for shape in shapes + ((2, 2, rows), (1, 1))),
-        in_specs=[any_spec] * 5,
-        out_specs=(any_spec,) * 5 + (vmem_spec,) * 2,
-        scratch_shapes=[vm(v.shape, v.dtype) for v in (grads, down, tok, gain, loss)]
-        + [vm(shape, F32) for shape in shapes]
-        + [pltpu.SemaphoreType.DMA((16,)), pltpu.SemaphoreType.DMA((16,))],
-        compiler_params=pltpu.CompilerParams(vmem_limit_bytes=62 * 2**20),
-    )(grads, down, tok, gain, loss)
+        in_specs=[vmem_spec] * 5,
+        out_specs=(pl.BlockSpec(memory_space=pl.ANY),) * 5 + (vmem_spec,) * 2,
+        scratch_shapes=[vm(shape, F32) for shape in shapes] + [pltpu.SemaphoreType.DMA((10,))],
+        compiler_params=pltpu.CompilerParams(vmem_limit_bytes=40 * 2**20),
+    )(*ins)
 
 
 def fused(tokens, positions, missing, qkv_weight, out_weight, up_weight, down_weight, norm_gains):

time: 127 us -> 114 us (0.90)
  Pallas kernels: 126 us -> 113 us
    pallas_call x1, Pallas kernels: 121 us -> 109 us  [layer_call(): pl.pallas_call(layer_kernel, out_shape=(vm((2, width // DP, n_chunks * CH...]
where the time goes in v3:
time: 114 us; the launch traced here: 113 us
  Pallas kernels  113 us (99%)
    pallas_call x1, Pallas kernels, layer_call(): pl.pallas_call(layer_kernel, out_shape=(vm((2, width // DP, n_chunks * CH...  109 us
    pallas_call x1, Pallas kernels, widen_call(): pl.pallas_call(widen_kernel, out_shape=tuple((jax.ShapeDtypeStruct(shape,...  3.97 us

profile of v3, /device:TPU:0, one launch (start us, length us, event | category | flops | bytes accessed | tf_op | source)
XLA Modules:
  0.0 113.3 jit_solution(539819758864042853)
XLA Ops:
  0.6 108.6 %shard_map.135 = (bf16[2,96,6144]{2,1,0:T(8,128)(2,1)S(1)}, bf16[2,384,768]{2,1,0:T(8,128)(2,1)S(1)}, bf16[2,192,768]{2,1,0:T(8,128)(2,1)S(1)}, f32[2,8,128]{2,1,0:T(8,128)S(1)}, f32[8,128]{1,0:T(8,128)S(1)}) custom-call(bf16[2,192,768]{2,1,0:T(8,128)(2,1)} %tokens.1, s32[2,96]{1,0:T(2,128)} %positions_h.1, s32[1,64]{1,0:T(1,128)} %bitcast.2, ...), custom_call_target="tpu_custom_call" | custom-call | tf_op jit(solution)/shard_map/pallas_call | solution.py:684
  109.2 4.0 %shard_map.136 = (f32[2,96,2304]{2,1,0:T(8,128)}, f32[2,96,768]{2,1,0:T(8,128)}, f32[2,96,3072]{2,1,0:T(8,128)}, f32[2,384,768]{2,1,0:T(8,128)}, f32[2,192,768]{...) custom-call(bf16[2,96,6144]{2,1,0:T(8,128)(2,1)S(1)} %get-tuple-element.19.grads, ...), custom_call_target="tpu_custom_call" | custom-call | tf_op jit(solution)/shard_map/pallas_call | solution.py:729

commit v4 on v3

--- a/solution.py
+++ b/solution.py
@@ -57,7 +57,7 @@
     grad_out, down_out, token_out, gain_out, loss_out,
     positions, missing, gains, wqkv, wout, wup, wdown, tok, posb, h_one, proj, probs, att, resid, h_two, slope,
     asum, rsum, pool, msg_a, recv_a, msg_b, send_b, recv_b, recv_b2, units, downs, downs_lo, ga, gp_own,
-    h_t, ht, gbuf, gatt, gh, gacc, recv_g, gx_send, gx_recv, as_mat,
+    h_t, ht, gbuf, gatt, gh, gacc, gsum, as_mat,
     ysend, keep, yrecv, ring_a, ring_b,
     load_sem, out_sem, ss, rs,
 ):
@@ -536,23 +536,67 @@
     tg_here = pltpu.make_async_copy(tok.at[own_rows(x)], token_out.at[x], load_sem.at[9])
     tg_here.start()
 
+    def gain_copy(src, dst, n, dev):
+        return rc(gsum.at[src], gsum.at[dst], S_G + n, dev)
+
+    g_core = gain_copy(0, 1, 0, core_dev)
+    g_y = gain_copy(2, 3, 1, y_dev)
+    g_oi = gain_copy(4, 5, 2, inward_peer)
+    g_ii = gain_copy(6, 7, 3, inner_peer)
+    g_io = gain_copy(8, 9, 4, outer_peer)
+    g_x = gain_copy(10, 11, 5, x_dev)
+    gsum[0] = jnp.zeros_like(gsum[0])
+    for n in range(2):
+        for q in range(pieces):
+            row = n * pieces + q
+            gsum[0, row : row + 1, :] = gacc[n : n + 1, q * lanes : (q + 1) * lanes]
+    g_core.start()
+
+    def gain_y():
+        g_core.wait_recv()
+        gsum[2] = gsum[0] + gsum[1]
+        g_y.start()
+
+    def gain_oi():
+        g_y.wait_recv()
+        gsum[4] = gsum[2] + gsum[3]
+
+        @pl.when(outer)
+        def _():
+            g_oi.start()
+
+    def gain_ii():
+        @pl.when(inner)
+        def _():
+            g_oi.wait_recv()
+            gsum[6] = gsum[5] + gsum[4]
+            g_ii.start()
+
+    def gain_io():
+        @pl.when(inner)
+        def _():
+            g_ii.wait_recv()
+            gsum[8] = gsum[7] + gsum[4]
+            g_io.start()
+            gsum[10] = gsum[7] + gsum[6]
+            g_x.start()
+
+    def gain_x():
+        @pl.when(outer)
+        def _():
+            g_io.wait_recv()
+            gsum[10] = gsum[4] + gsum[9]
+            g_x.start()
+
     comm(8)
     for cp in ht_copies[8:12]:
         cp.wait_recv()
     for n in range(3):
         wgrad(n_wide + 1 + n, 2)
+        if n == 0:
+            gain_y()
         comm(9 + n)
 
-    gx_send[...] = jnp.zeros_like(gx_send)
-    for n in range(2):
-        for q in range(pieces):
-            row = n * pieces + q
-            gx_send[0, row : row + 1, :] = gacc[n : n + 1, q * lanes : (q + 1) * lanes]
-    recv_g[x, yz] = gx_send[0]
-    g_copies = []
-    for k, yy, xx, zz in others():
-        g_copies.append(rc(recv_g.at[x, yz], recv_g.at[x, yz], S_G + k, at(yy, xx, c, zz)))
-        g_copies[-1].start()
     comm(12)
 
     for cp in b_copies:
@@ -578,22 +622,20 @@
         comm(t)
         return carry
 
-    lax.fori_loop(15, n_chunks + 3, drain, 0)
-    for cp in g_copies:
-        cp.wait_recv()
-    for m in range(2):
-        total = recv_g[m, 0]
-        for n in range(1, 8):
-            total = total + recv_g[m, n]
-        gx_send[m] = total
-    gx_copy = rc(gx_send, gx_recv, S_GX, core_dev)
-    gx_copy.start()
-    lax.fori_loop(n_chunks + 3, n_chunks + 6, drain, 0)
-    gx_copy.wait_recv()
-    total = gx_send[...] + gx_recv[...]
-    for m in range(2):
+    lax.fori_loop(15, 20, drain, 0)
+    gain_oi()
+    lax.fori_loop(20, 22, drain, 0)
+    gain_ii()
+    lax.fori_loop(22, n_chunks, drain, 0)
+    gain_io()
+    lax.fori_loop(n_chunks, n_chunks + 2, drain, 0)
+    gain_x()
+    lax.fori_loop(n_chunks + 2, n_chunks + 6, drain, 0)
+    g_x.wait_recv()
+    for m, n in ((x, 10), (1 - x, 11)):
+        total = gsum[n]
         flat = jnp.concatenate(
-            [jnp.concatenate([total[m, n * pieces + q : n * pieces + q + 1] for q in range(pieces)], axis=1) for n in range(2)],
+            [jnp.concatenate([total[r * pieces + q : r * pieces + q + 1] for q in range(pieces)], axis=1) for r in range(2)],
             axis=0,
         )
         share = width // DP
@@ -619,8 +661,18 @@
         return carry
 
     lax.fori_loop(0, n_chunks, finish, 0)
-    for cp in a_copies + b_copies + ht_copies + g_copies + [tok_send, pos_send, ax_copy, bx_copy, gx_copy]:
+    for cp in a_copies + b_copies + ht_copies + [tok_send, pos_send, ax_copy, bx_copy, g_core, g_y, g_x]:
         cp.wait_send()
+
+    @pl.when(outer)
+    def _():
+        g_oi.wait_send()
+
+    @pl.when(inner)
+    def _():
+        g_ii.wait_send()
+        g_io.wait_send()
+
     for j in range(n_blocks):
         gb_copy(j).wait_send()
     tg_copy.wait()
@@ -671,9 +723,7 @@
         vm((rows, width), BF16),
         vm((rows, width), F32),
         vm((8, width), F32),
-        vm((2, 8, 16, 128), F32),
-        vm((2, 16, 128), F32),
-        vm((2, 16, 128), F32),
+        vm((12, 16, 128), F32),
         vm((items, hidden // DP), BF16),
         vm(piece, BF16), vm(piece, BF16), vm(piece, BF16), vm(piece, BF16), vm(piece, BF16),
         pltpu.SemaphoreType.DMA((12,)),

time: 114 us -> 111 us (0.974)
  Pallas kernels: 113 us -> 110 us
    pallas_call x1, Pallas kernels: 109 us -> 106 us  [layer_call(): pl.pallas_call(layer_kernel, out_shape=(vm((2, width // DP, n_chunks * CH...]
where the time goes in v4:
time: 111 us
  Pallas kernels  110 us (99%)
    pallas_call x1, Pallas kernels, layer_call(): pl.pallas_call(layer_kernel, out_shape=(vm((2, width // DP, n_chunks * CH...  106 us
    pallas_call x1, Pallas kernels, widen_call(): pl.pallas_call(widen_kernel, out_shape=tuple((jax.ShapeDtypeStruct(shape,...  3.97 us

profile of v4, /device:TPU:0, one launch (start us, length us, event | category | flops | bytes accessed | tf_op | source)
XLA Modules:
  0.0 111.0 jit_solution(8802087485085590513)
XLA Ops:
  0.6 106.3 %shard_map.135 = (bf16[2,96,6144]{2,1,0:T(8,128)(2,1)S(1)}, bf16[2,384,768]{2,1,0:T(8,128)(2,1)S(1)}, bf16[2,192,768]{2,1,0:T(8,128)(2,1)S(1)}, f32[2,8,128]{2,1,0:T(8,128)S(1)}, f32[8,128]{1,0:T(8,128)S(1)}) custom-call(bf16[2,192,768]{2,1,0:T(8,128)(2,1)} %tokens.1, s32[2,96]{1,0:T(2,128)} %positions_h.1, s32[1,64]{1,0:T(1,128)} %bitcast.2, ...), custom_call_target="tpu_custom_call" | custom-call | tf_op jit(solution)/shard_map/pallas_call | solution.py:734
  106.9 4.0 %shard_map.136 = (f32[2,96,2304]{2,1,0:T(8,128)}, f32[2,96,768]{2,1,0:T(8,128)}, f32[2,96,3072]{2,1,0:T(8,128)}, f32[2,384,768]{2,1,0:T(8,128)}, f32[2,192,768]{...) custom-call(bf16[2,96,6144]{2,1,0:T(8,128)(2,1)S(1)} %get-tuple-element.19.grads, ...), custom_call_target="tpu_custom_call" | custom-call | tf_op jit(solution)/shard_map/pallas_call | solution.py:779

commit v5 on v4

--- a/solution.py
+++ b/solution.py
@@ -59,7 +59,7 @@
     asum, rsum, pool, msg_a, recv_a, msg_b, send_b, recv_b, recv_b2, units, downs, downs_lo, ga, gp_own,
     h_t, ht, gbuf, gatt, gh, gacc, gsum, as_mat,
     ysend, keep, yrecv, ring_a, ring_b,
-    load_sem, out_sem, ss, rs,
+    load_sem, ss, rs,
 ):
     width = h_one.shape[1]
     hidden = wup.shape[1]
@@ -124,6 +124,9 @@
     for load in loads[: len(early)]:
         load.start()
     load_pos, load_tok, load_gains, load_qkv, load_missing, load_out, load_up, load_down = loads
+    pl.semaphore_wait(barrier, 16)
+    tok_send = rc(tokens.at[1 - x], tok.at[own_rows(x)], S_TOK, x_dev)
+    tok_send.start()
     posb[x] = jnp.zeros((8, lanes), F32)
     asum[...] = jnp.zeros_like(asum)
     rsum[...] = jnp.zeros_like(rsum)
@@ -137,10 +140,7 @@
     posb[x, 0:2, 0:patches] = cell_rows
     posb[x, 2:4, 0:patches] = cell_cols
 
-    pl.semaphore_wait(barrier, 16)
-    tok_send = rc(tokens.at[1 - x], tok.at[own_rows(x)], S_TOK, x_dev)
     pos_send = rc(posb.at[x], posb.at[x], S_POS, x_dev)
-    tok_send.start()
     pos_send.start()
 
     low_lanes = lax.broadcasted_iota(jnp.int32, (patches, lanes), 1) < lanes // 2
@@ -187,7 +187,7 @@
                 att[r, p * lanes : (p + 1) * lanes] = fold_heads(nn_dot(soft[p], v)).astype(BF16)
             return carry
 
-        lax.fori_loop(0, 2, image, 0)
+        lax.fori_loop(0, 2, image, 0, unroll=True)
 
     def wide(j):
         return pl.ds(pl.multiple_of(j * width, width), width)
@@ -379,11 +379,9 @@
             grad_out.at[x, :, out_cols(k)], S_X + k, x_dev,
         )
 
-    def here_copy(k):
-        return pltpu.make_async_copy(
-            yrecv.at[k, pl.ds(pl.multiple_of(x * quarter, quarter), quarter), :],
-            grad_out.at[x, :, out_cols(k)], out_sem.at[k],
-        )
+    def store_here(k):
+        here = pl.ds(pl.multiple_of(x * quarter, quarter), quarter)
+        grad_out[x, :, out_cols(k)] = yrecv[k, here, :]
 
     def step_y(k):
         y_copy(k).wait_recv()
@@ -409,7 +407,7 @@
             io_copy(k).start()
             yrecv[k] = (got + ring_a[k].astype(F32)).astype(BF16)
             x_copy(k).start()
-            here_copy(k).start()
+            store_here(k)
 
     def step_c(k):
         @pl.when(outer)
@@ -417,7 +415,7 @@
             io_copy(k).wait_recv()
             yrecv[k] = (keep[k].astype(F32) + ring_a[k].astype(F32)).astype(BF16)
             x_copy(k).start()
-            here_copy(k).start()
+            store_here(k)
 
     def comm(t):
         for lag, step in ((0, step_y), (2, step_a), (4, step_b), (6, step_c)):
@@ -618,10 +616,28 @@
         down_out[m] = tn_dot(as_mat[...], downs[m]).astype(BF16)
     comm(14)
 
+    def finish(k, carry):
+        y_copy(k).wait_send()
+        x_copy(k).wait()
+
+        @pl.when(outer)
+        def _():
+            oi_copy(k).wait_send()
+
+        @pl.when(inner)
+        def _():
+            ii_copy(k).wait_send()
+            io_copy(k).wait_send()
+
+        return carry
+
+    behind = 10
+
     def drain(t, carry):
         comm(t)
-        return carry
-
+        return finish(t - behind, carry)
+
+    lax.fori_loop(0, 15 - behind, finish, 0)
     lax.fori_loop(15, 20, drain, 0)
     gain_oi()
     lax.fori_loop(20, 22, drain, 0)
@@ -644,23 +660,7 @@
             own = jnp.where(dp == d, flat[:, d * share : (d + 1) * share], own)
         gain_out[m, 0:2, 0:share] = own
 
-    def finish(k, carry):
-        y_copy(k).wait_send()
-        here_copy(k).wait()
-        x_copy(k).wait()
-
-        @pl.when(outer)
-        def _():
-            oi_copy(k).wait_send()
-
-        @pl.when(inner)
-        def _():
-            ii_copy(k).wait_send()
-            io_copy(k).wait_send()
-
-        return carry
-
-    lax.fori_loop(0, n_chunks, finish, 0)
+    lax.fori_loop(n_chunks + 6 - behind, n_chunks, finish, 0)
     for cp in a_copies + b_copies + ht_copies + [tok_send, pos_send, ax_copy, bx_copy, g_core, g_y, g_x]:
         cp.wait_send()
 
@@ -727,7 +727,6 @@
         vm((items, hidden // DP), BF16),
         vm(piece, BF16), vm(piece, BF16), vm(piece, BF16), vm(piece, BF16), vm(piece, BF16),
         pltpu.SemaphoreType.DMA((12,)),
-        pltpu.SemaphoreType.DMA((n_chunks,)),
         pltpu.SemaphoreType.DMA((n_sems,)),
         pltpu.SemaphoreType.DMA((n_sems,)),
     ]

time: 111 us -> 110 us (level)
  no operation moved by 1% of the time
where the time goes in v5:
time: 110 us
  Pallas kernels  110 us (100%)
    pallas_call x1, Pallas kernels, layer_call(): pl.pallas_call(layer_kernel, out_shape=(vm((2, width // DP, n_chunks * CH...  106 us
    pallas_call x1, Pallas kernels, widen_call(): pl.pallas_call(widen_kernel, out_shape=tuple((jax.ShapeDtypeStruct(shape,...  3.97 us

profile of v5, /device:TPU:0, one launch (start us, length us, event | category | flops | bytes accessed | tf_op | source)
XLA Modules:
  0.0 110.3 jit_solution(779310774302321596)
XLA Ops:
  0.6 105.6 %shard_map.135 = (bf16[2,96,6144]{2,1,0:T(8,128)(2,1)S(1)}, bf16[2,384,768]{2,1,0:T(8,128)(2,1)S(1)}, bf16[2,192,768]{2,1,0:T(8,128)(2,1)S(1)}, f32[2,8,128]{2,1,0:T(8,128)S(1)}, f32[8,128]{1,0:T(8,128)S(1)}) custom-call(bf16[2,192,768]{2,1,0:T(8,128)(2,1)} %tokens.1, s32[2,96]{1,0:T(2,128)} %positions_h.1, s32[1,64]{1,0:T(1,128)} %bitcast.2, ...), custom_call_target="tpu_custom_call" | custom-call | tf_op jit(solution)/shard_map/pallas_call | solution.py:733
  106.2 4.0 %shard_map.136 = (f32[2,96,2304]{2,1,0:T(8,128)}, f32[2,96,768]{2,1,0:T(8,128)}, f32[2,96,3072]{2,1,0:T(8,128)}, f32[2,384,768]{2,1,0:T(8,128)}, f32[2,192,768]{...) custom-call(bf16[2,96,6144]{2,1,0:T(8,128)(2,1)S(1)} %get-tuple-element.19.grads, ...), custom_call_target="tpu_custom_call" | custom-call | tf_op jit(solution)/shard_map/pallas_call | solution.py:778
